TPU v7x, 32 devices: a whole 2x2x4 slice. The times are simulated.
32 devices in a mesh: ctx: 8 (over z, x), heads: 4 (over y, core).
Axes of the slice: x: 2, y: 2, z: 4, core: 2. Of those that a mesh axis runs over, the one named last changes fastest.
Arguments:
- q_raw: bfloat16 [2048, 8192], P('ctx', 'heads'), may hold values from -60 to 60
- k_raw: bfloat16 [2048, 1024], P('ctx', 'heads'), may hold values from -60 to 60
- values: bfloat16 [2048, 1024], P('ctx', 'heads'), may hold values from -6 to 6
- saved_out: bfloat16 [2048, 8192], P('ctx', 'heads'), may hold values from -6 to 6
- out_grad: bfloat16 [2048, 8192], P('ctx', 'heads'), may hold values from -60 to 60
- q_gain: float32 [128], replicated, may hold values from 0.25 to 1.75
- k_gain: float32 [128], replicated, may hold values from 0.25 to 1.75
- ancestors: int32 [32, 32], P('ctx'), may hold values from -1 to 31, as said below
Outputs:
- dq_raw: bfloat16 [2048, 8192], P('ctx', 'heads')
- dk_raw: bfloat16 [2048, 1024], P('ctx', 'heads')
- dv: bfloat16 [2048, 1024], P('ctx', 'heads')
- q_gain_grad: float32 [128], replicated
- k_gain_grad: float32 [128], replicated
Inputs may be any that keep to these rules, and one draw needn't show every extreme that they name: `ancestors`: the forest is 1 trees of 32 blocks each; in tree order, tree k holds blocks (k * 32 + 256 / 64 + b) mod 32 for b = 0 to 31. Row b lists, in tree order, every block on the path from its tree's first block to b, ending with b itself, then -1s. The first 16 blocks of a tree form its prompt, each the child of the block before it; every other block's parent is a block earlier in its tree, from the prompt's last block on.
All inputs are finite; a program needn't handle non-finite values.
Results may differ from a plain program's by a relative error of at most 0.0069.
Values may be sent and summed in bfloat16 or wider, within the bound.
No kernel may reach another device: no remote copies, remote signals or barrier semaphores. Data moves between devices by JAX's collectives and lax.ppermute only.
A program may use at most 64 MiB of HBM per device.

v0:
```python
import math

import jax
import jax.numpy as jnp
import numpy as np
from jax import lax
from jax.experimental import pallas as pl
from jax.experimental.pallas import tpu as pltpu
from jax.sharding import PartitionSpec as P

ROPE_BASE = 1000000.0
EPS = 1e-06
HIDDEN = -100000.0
VMEM_LIMIT = 16 * 1024 * 1024
ATTEND_VMEM_LIMIT = 34 * 1024 * 1024
F32 = jnp.float32
BF16 = jnp.bfloat16


def rope_rows(starts, head_dim):
    half = head_dim // 2
    frequency = np.exp(
        np.arange(half, dtype=np.float32) * np.float32(-2.0 * math.log(ROPE_BASE) / head_dim)
    ).astype(np.float32)
    angles = np.asarray(starts, np.float32)[:, None] * frequency[None, :]
    cos = np.cos(angles.astype(np.float64)).astype(np.float32)
    sin = np.sin(angles.astype(np.float64)).astype(np.float32)
    return np.concatenate([cos, cos], 1), np.concatenate([-sin, sin], 1)


def block_tables(depth, tables):
    start_cos, start_sin, offset_cos, offset_sin = tables
    cos, sin = start_cos[pl.ds(depth, 1), :], start_sin[pl.ds(depth, 1), :]
    both_cos = cos * offset_cos[...] - sin * offset_sin[...]
    both_sin = sin * offset_cos[...] + cos * offset_sin[...]
    return both_cos, both_sin


def turned(rows, cos, sin):
    return rows * cos + pltpu.roll(rows, rows.shape[-1] // 2, 1) * sin


def turned_back(rows, cos, sin):
    return rows * cos - pltpu.roll(rows, rows.shape[-1] // 2, 1) * sin


def inverse_rms(rows):
    return lax.rsqrt(jnp.mean(rows * rows, -1, keepdims=True) + EPS)


def own_tables(depth_ref, tables, blocks):
    parts = [block_tables(depth_ref[a], tables) for a in range(blocks)]
    return jnp.concatenate([p[0] for p in parts], 0), jnp.concatenate([p[1] for p in parts], 0)


def dot_nn(lhs, rhs):
    return lax.dot_general(lhs, rhs, (((1,), (0,)), ((), ())), preferred_element_type=F32)


def plan_kernel(blocks, tree_dev, place_ref, anc_ref, plan_ref):
    slots = tree_dev * blocks
    place = place_ref[0]
    here = jnp.where(place + 1 == tree_dev, 0, place + 1)
    for row in range(4):
        for i in range(slots):
            plan_ref[row, i] = 0
    count = jnp.int32(blocks)
    steps = [jnp.int32(0)] * blocks
    for b in range(slots):
        bits = jnp.int32(0)
        depth = jnp.int32(0)
        for a in range(blocks):
            hit = anc_ref[a, jnp.minimum(steps[a], slots - 1)] == b
            bits = bits | jnp.where(hit, 1 << a, 0)
            depth = jnp.where(hit, steps[a], depth)
            steps[a] = steps[a] + jnp.where(hit, 1, 0)
        own = place == b // blocks
        slot = jnp.where(own, b % blocks, jnp.minimum(count, slots - 1))
        there = (b // blocks + 1) % tree_dev
        odd = jnp.bitwise_and(here + there, 1)
        gap = jnp.bitwise_xor(here, odd) - there
        gap = jnp.where(gap < 0, gap + tree_dev, gap)
        plan_ref[0, slot] = odd * (tree_dev // 2) + lax.shift_right_logical(gap, 1)
        plan_ref[1, slot] = b % blocks
        plan_ref[2, slot] = depth
        plan_ref[3, slot] = bits
        count = count + jnp.where(own | (bits == 0), 0, 1)
    for i in range(slots):
        plan_ref[4, i] = count


def prep_kernel(blocks, block_len, kv_heads, depth_ref, t0, t1, t2, t3, gain_ref, q_ref, grad_ref, out_ref, *outs):
    tokens = q_ref.shape[0]
    head_dim = gain_ref.shape[1]
    cos, sin = own_tables(depth_ref, (t0, t1, t2, t3), blocks)
    gain = gain_ref[...]
    group = q_ref.shape[1] // head_dim // kv_heads
    for head in range(group * kv_heads):
        g = head % group
        q_t_ref, q_rot_ref, grad_t_ref, grad_heads_ref, delta_ref = outs[5 * (head // group):][:5]
        cols = pl.ds(head * head_dim, head_dim)
        here = pl.ds(g * tokens, tokens)
        rows = q_ref[:, cols].astype(F32)
        rotated = turned(rows * inverse_rms(rows) * gain, cos, sin)
        q_rot_ref[here, :] = rotated.astype(BF16)
        q_t_ref[:, here] = jnp.transpose(rotated).astype(BF16)
        grad = grad_ref[:, cols]
        grad_heads_ref[here, :] = grad
        grad_rows = jnp.transpose(grad.astype(F32))
        grad_t_ref[:, here] = grad_rows.astype(BF16)
        product = grad_rows * jnp.transpose(out_ref[:, cols].astype(F32))
        delta_ref[:, here] = jnp.sum(product, 0, keepdims=True)


def main_kernel(blocks, block_len, tree_dev, inv_root, n_in, last, *refs):
    plan_ref, gain_ref = refs[:2]
    tables = refs[2:6]
    half = tree_dev // 2
    pieces, crossed_ref = refs[6:5 + n_in], refs[5 + n_in]
    q_t_ref, q_ref, grad_t_ref, grad_ref, delta_ref = refs[6 + n_in:11 + n_in]
    dq_ref, gain_part_ref = refs[11 + n_in:13 + n_in]
    parts = refs[13 + n_in:13 + n_in + half + last]
    crossed_part, raw, keys, keys_t, vals, shown, with_cos, with_sin, expo, mass, w_even, ds_even, w_odd, ds_odd, found, spread = refs[
        13 + n_in + half + last:]
    head_dim = gain_ref.shape[1]
    tokens = raw.shape[1]
    group = q_ref.shape[0] // tokens
    count = plan_ref[4, 0]
    chunks = (count + blocks - 1) // blocks
    gain = gain_ref[...]
    for i, piece in enumerate(pieces):
        raw[i] = piece[...]
    raw[len(pieces):] = crossed_ref[...]
    query_block = lax.broadcasted_iota(jnp.int32, (1, tokens), 1) // block_len

    def rows_of(start):
        return pl.ds(pl.multiple_of(start * block_len, block_len), block_len)

    def load_chunk(c):
        for j in range(blocks):
            slot = jnp.minimum(c * blocks + j, tree_dev * blocks - 1)
            piece = plan_ref[0, slot]
            rows = rows_of(plan_ref[1, slot])
            cos, sin = block_tables(plan_ref[2, slot], tables)
            unit = raw[piece, rows, 0:head_dim].astype(F32)
            unit = unit * inverse_rms(unit)
            here = pl.ds(j * block_len, block_len)
            with_cos[c, here, :] = unit * cos
            with_sin[c, here, :] = pltpu.roll(unit * sin, head_dim // 2, 1)
            keys[c, here, :] = turned(unit * gain, cos, sin).astype(BF16)
            bits = jnp.where(c * blocks + j < count, plan_ref[3, slot], 0)
            row = jnp.zeros((1, tokens), F32)
            for a in range(blocks):
                seen = lax.rem(lax.shift_right_logical(bits, a), 2)
                row = jnp.where((query_block == a) & (seen == 0), HIDDEN, row)
            shown[c, j:j + 1, :] = row
            vals[c, here, :] = raw[piece, rows, head_dim:]
        keys_t[c] = jnp.transpose(keys[c].astype(F32)).astype(BF16)

    def exps(c, g, scores):
        parts = []
        for j in range(blocks):
            here = slice(j * block_len, (j + 1) * block_len)
            parts.append(jnp.exp(scores[here] * inv_root + shown[c, j:j + 1, :]))
        return jnp.concatenate(parts, 0)

    def summed(e):
        return jnp.sum(e.reshape(tokens // 8, 8, tokens), 0)

    key_row = lax.broadcasted_iota(jnp.int32, (tokens, tokens), 0)
    query_col = lax.broadcasted_iota(jnp.int32, (tokens, tokens), 1)

    def cols_of(g):
        return pl.ds(g * tokens, tokens)

    def masses(c, first):
        for g in range(group):
            scores = dot_nn(keys[c], q_t_ref[:, cols_of(g)])
            e = exps(c, g, scores)
            if first:
                e = jnp.where(key_row <= query_col, e, 0.0)
            expo[c, g] = e
            mass[g] = summed(e) if first else mass[g] + summed(e)

    load_chunk(0)
    masses(0, True)
    load_chunk(1)

    @pl.loop(1, chunks)
    def _(c):
        masses(c, False)
        load_chunk(c + 1)

    for g in range(group):
        total = jnp.sum(mass[g], 0, keepdims=True)
        mass[g] = jnp.broadcast_to(1.0 / total, (8, tokens))
    dq_ref[...] = jnp.zeros(dq_ref.shape, F32)
    gain_part_ref[...] = jnp.zeros(gain_part_ref.shape, F32)
    spread[...] = jnp.zeros(spread.shape, BF16)

    def weigh(c, heads, w_all, ds_all):
        for g in heads:
            cols = cols_of(g)
            grad_prob = dot_nn(vals[c], grad_t_ref[:, cols])
            weights = expo[c, g] * mass[g, 0:1, :]
            ds_all[:, cols] = (weights * (grad_prob - delta_ref[:, cols])).astype(BF16)
            w_all[:, cols] = weights.astype(BF16)

    def value_products(c, w_all):
        found[c, :, head_dim:] = dot_nn(w_all[...], grad_ref[...]).astype(BF16)

    def key_products(c, ds_all):
        dk = dot_nn(ds_all[...], q_ref[...]) * inv_root
        found[c, :, 0:head_dim] = dk.astype(BF16)
        front = jnp.sum((dk * with_cos[c]).reshape(tokens // 8, 8, head_dim), 0)
        back = jnp.sum((dk * with_sin[c]).reshape(tokens // 8, 8, head_dim), 0)
        gain_part_ref[...] = gain_part_ref[...] + front - pltpu.roll(back, head_dim // 2, 1)

    def query_products(c, ds_all):
        dq_ref[...] = dq_ref[...] + dot_nn(keys_t[c], ds_all[...])

    thirds = [range(group * i // 3, group * (i + 1) // 3) for i in range(3)]
    buffers = ((w_even, ds_even), (w_odd, ds_odd))

    def products(c, now):
        value_products(c, now[0])
        key_products(c, now[1])
        query_products(c, now[1])

    def step(c, now, later):
        value_products(c, now[0])
        weigh(c + 1, thirds[0], *later)
        key_products(c, now[1])
        weigh(c + 1, thirds[1], *later)
        query_products(c, now[1])
        weigh(c + 1, thirds[2], *later)

    weigh(0, range(group), *buffers[0])

    @pl.loop(0, (chunks - 1) // 2)
    def _(pair):
        step(2 * pair, buffers[0], buffers[1])
        step(2 * pair + 1, buffers[1], buffers[0])

    odd_count = lax.rem(chunks, 2) == 1

    @pl.when(odd_count)
    def _():
        products(chunks - 1, buffers[0])

    @pl.when(jnp.logical_not(odd_count))
    def _():
        step(chunks - 2, buffers[0], buffers[1])
        products(chunks - 1, buffers[1])

    @pl.loop(0, count)
    def _(slot):
        rows = rows_of(lax.rem(slot, blocks))
        spread[plan_ref[0, slot], rows_of(plan_ref[1, slot]), :] = found[slot // blocks, rows, :]

    for piece in range(half + last):
        parts[piece][...] = spread[piece]
    crossed_part[...] = spread[half + last:]


def join_kernel(*refs):
    for i in range(refs[-1].shape[0]):
        refs[-1][i] = refs[i][...]


def merge_kernel(*refs):
    count = (len(refs) - 5) // 2
    parts, (near_ref, others_ref, gains_ref, before_ref) = refs[:count], refs[count:count + 4]
    outs, (near_out_ref, joined_ref, gains_out_ref) = refs[count + 4:-3], refs[-3:]
    for i in range(count):
        both = (parts[i][...].astype(F32) + others_ref[i].astype(F32)).astype(BF16)
        if i < count - 1:
            outs[i][...] = both
        else:
            joined_ref[joined_ref.shape[0] - 1] = both
    for head in range(joined_ref.shape[0] - 1):
        joined_ref[head] = before_ref[head]
    near_out_ref[...] = near_ref[...]
    gains_out_ref[...] = gains_ref[...]


def query_kernel(blocks, inv_root, kv_heads, depth_ref, t0, t1, t2, t3, gain_ref, q_ref, *refs):
    dq_refs, (k_part_refs, (out_ref, gains_ref)) = refs[:kv_heads], (refs[kv_heads:-2], refs[-2:])
    tokens = q_ref.shape[0]
    head_dim = gain_ref.shape[1]
    group = dq_refs[0].shape[1] // tokens
    cos, sin = own_tables(depth_ref, (t0, t1, t2, t3), blocks)
    gain = gain_ref[...]
    part = jnp.zeros((8, head_dim), F32)
    for head in range(group * len(dq_refs)):
        cols = pl.ds(head * head_dim, head_dim)
        rows = q_ref[:, cols].astype(F32)
        recip = inverse_rms(rows)
        normed = rows * recip
        dq = jnp.transpose(dq_refs[head // group][:, pl.ds(head % group * tokens, tokens)])
        scaled_grad = turned_back(dq, cos, sin) * inv_root
        term = scaled_grad * normed
        part = part + jnp.sum(term.reshape(tokens // 8, 8, head_dim), 0)
        inner = jnp.mean(term * gain, -1, keepdims=True)
        out_ref[:, cols] = (recip * (scaled_grad * gain - normed * inner)).astype(BF16)
    k_part = sum(ref[...] for ref in k_part_refs)
    gains = jnp.concatenate([jnp.sum(part, 0, keepdims=True), jnp.sum(k_part, 0, keepdims=True)], 0)
    gains_ref[...] = jnp.broadcast_to(gains[None], gains_ref.shape)


def summed_terms(refs, places):
    total = 0.0
    for ref, place in zip(refs, places):
        total = total + (ref[...] if place is None else ref[place]).astype(F32)
    return total


def early_kernel(places, gains_ref, *refs):
    terms, (sum_ref, gains_out_ref) = refs[:-2], refs[-2:]
    sum_ref[...] = summed_terms(terms, places)
    gains_out_ref[...] = gains_ref[...]


def key_kernel(blocks, places, depth_ref, t0, t1, t2, t3, gain_ref, k_ref, gains_ref, *refs):
    terms, (dk_out_ref, dv_out_ref, total_ref) = refs[:-3], refs[-3:]
    total_ref[...] = jnp.sum(gains_ref[...], 0)
    head_dim = gain_ref.shape[1]
    cos, sin = own_tables(depth_ref, (t0, t1, t2, t3), blocks)
    gain = gain_ref[...]
    for head, mine in enumerate(places):
        cols = pl.ds(head * head_dim, head_dim)
        rows = k_ref[:, cols].astype(F32)
        recip = inverse_rms(rows)
        normed = rows * recip
        both = summed_terms(terms[:len(mine)], mine)
        terms = terms[len(mine):]
        grad = turned_back(both[:, 0:head_dim], cos, sin) * gain
        inner = jnp.mean(grad * normed, -1, keepdims=True)
        dk_out_ref[:, cols] = (recip * (grad - normed * inner)).astype(BF16)
        dv_out_ref[:, cols] = both[:, head_dim:].astype(BF16)


class Tree:
    def __init__(self, size, cycle):
        self.size, self.cycle = size, cycle

    def order(self, index):
        return (index - 1) % self.size

    def send(self, value, target, wanted):
        pairs = []
        for tree in range(self.cycle // self.size):
            for index in range(self.size):
                if wanted(index):
                    ends = [(tree * self.size + 1 + self.order(i)) % self.cycle for i in (index, target(index))]
                    pairs.append(tuple(ends))
        return lax.ppermute(value, "ctx", pairs)

    def after(self, *pair):
        return self.order(pair[1] % self.size) > self.order(pair[0] % self.size)

    def along(self, own):
        pieces = []
        for step in range(2, self.size, 2):
            there = lambda i: (i + step) % self.size
            pieces.append(self.send(own, there, lambda i: self.after(i, there(i)) or self.after(i, there(i) ^ 1)))
        return pieces

    def across(self, value, steps, back=False):
        if back:
            return self.send(value, lambda i: i ^ 1, lambda i: any(self.after((i ^ 1) - step, i) for step in steps))
        return self.send(value, lambda i: i ^ 1, lambda i: any(self.after(i - step, i ^ 1) for step in steps))

    def home(self, value, step):
        there = lambda i: (i - step) % self.size
        return self.send(value, there, lambda i: self.after(there(i), i) or self.after(there(i), i ^ 1))


def on_device(q_raw, k_raw, values, saved_out, out_grad, q_gain, k_gain, ancestors):
    tokens = q_raw.shape[0]
    head_dim = q_gain.shape[0]
    kv_heads = k_raw.shape[1] // head_dim
    heads = q_raw.shape[1] // head_dim
    group = heads // kv_heads
    blocks = ancestors.shape[0]
    tree_blocks = ancestors.shape[1]
    block_len = tokens // blocks
    tree_dev = tree_blocks // blocks
    cycle = lax.axis_size("ctx")
    inv_root = 1.0 / math.sqrt(head_dim)
    tree = Tree(tree_dev, cycle)
    place = (lax.axis_index("ctx") - 1 + cycle) % cycle % tree_dev
    place = place.reshape(1).astype(jnp.int32)

    depth = jnp.sum((ancestors >= 0).astype(jnp.int32), 1) - 1
    total_blocks = blocks * cycle
    in_tree = jnp.where(
        ancestors >= 0, (ancestors - blocks + total_blocks) % total_blocks % tree_blocks, -1
    )
    tables = [
        jnp.asarray(table)
        for starts in (range(0, tree_blocks * block_len, block_len), range(block_len))
        for table in rope_rows(starts, head_dim)
    ]
    q_gain_row, k_gain_row = q_gain.reshape(1, head_dim), k_gain.reshape(1, head_dim)

    steps = range(2, tree_dev, 2)
    own = []
    for h in range(kv_heads):
        cols = slice(h * head_dim, (h + 1) * head_dim)
        own.append(jnp.concatenate([k_raw[:, cols], values[:, cols]], 1))

    params = pltpu.CompilerParams(vmem_limit_bytes=VMEM_LIMIT)
    smem = pl.BlockSpec(memory_space=pltpu.SMEM)
    vmem = pl.BlockSpec(memory_space=pltpu.VMEM)
    sds = jax.ShapeDtypeStruct
    slow = pl.CostEstimate(flops=4 * 10**9, bytes_accessed=16 * 1024 * 1024, transcendentals=0)
    quick = pl.CostEstimate(flops=1024, bytes_accessed=1024, transcendentals=0)

    plan = pl.pallas_call(
        lambda *refs: plan_kernel(blocks, tree_dev, *refs),
        out_shape=sds((5, tree_blocks), jnp.int32),
        in_specs=[smem, smem],
        out_specs=smem,
        cost_estimate=quick,
        name="plan",
    )(place, in_tree)

    def join(arrays, *after):
        count = len(arrays)
        return pl.pallas_call(
            join_kernel,
            out_shape=sds((count, tokens, 2 * head_dim), BF16),
            in_specs=[vmem] * count + [pl.BlockSpec(memory_space=pl.ANY)] * len(after),
            out_specs=vmem,
            compiler_params=params,
            cost_estimate=quick,
            name="join",
        )(*arrays, *after)

    rows = group * tokens
    queries = pl.pallas_call(
        lambda *refs: prep_kernel(blocks, block_len, kv_heads, *refs),
        out_shape=tuple(
            [
                sds((head_dim, rows), BF16),
                sds((rows, head_dim), BF16),
                sds((head_dim, rows), BF16),
                sds((rows, head_dim), BF16),
                sds((1, rows), F32),
            ]
            * kv_heads
        ),
        in_specs=[smem] + [vmem] * 8,
        out_specs=tuple([vmem] * (5 * kv_heads)),
        compiler_params=params,
        cost_estimate=slow,
        name="prep",
    )(depth, *tables, q_gain_row, q_raw, out_grad, saved_out)

    pieces = []
    for h in range(kv_heads):
        straight = tree.along(own[h])
        if h == 0:
            cross = [tree.across(own[h], [0])]
            crossed = tree.across(join(straight, cross[0], plan), steps)
        else:
            cross = []
            crossed = tree.across(join([own[h], *straight], queries[4], queries[-1]), [0, *steps])
        pieces.append([own[h], *straight, *cross, crossed])

    half = tree_dev // 2

    def attend(h):
        last = h == kv_heads - 1
        return pl.pallas_call(
            lambda *refs: main_kernel(blocks, block_len, tree_dev, inv_root, len(pieces[h]), last, *refs),
            out_shape=(
                sds((head_dim, rows), F32),
                sds((8, head_dim), F32),
                *[sds((tokens, 2 * head_dim), BF16)] * (half + last),
                sds((half - last, tokens, 2 * head_dim), BF16),
            ),
            in_specs=[smem] + [vmem] * (10 + len(pieces[h])),
            out_specs=tuple([vmem] * (3 + half + last)),
            scratch_shapes=[
                pltpu.VMEM((tree_dev, tokens, 2 * head_dim), BF16),
                pltpu.VMEM((tree_dev + 1, tokens, head_dim), BF16),
                pltpu.VMEM((tree_dev + 1, head_dim, tokens), BF16),
                pltpu.VMEM((tree_dev + 1, tokens, head_dim), BF16),
                pltpu.VMEM((tree_dev + 1, 8 * ((blocks + 7) // 8), tokens), F32),
                pltpu.VMEM((tree_dev + 1, tokens, head_dim), F32),
                pltpu.VMEM((tree_dev + 1, tokens, head_dim), F32),
                pltpu.VMEM((tree_dev, group, tokens, tokens), F32),
                pltpu.VMEM((group, 8, tokens), F32),
                *[pltpu.VMEM((tokens, rows), BF16)] * 4,
                pltpu.VMEM((tree_dev, tokens, 2 * head_dim), BF16),
                pltpu.VMEM((tree_dev, tokens, 2 * head_dim), BF16),
            ],
            compiler_params=pltpu.CompilerParams(vmem_limit_bytes=ATTEND_VMEM_LIMIT),
            cost_estimate=pl.CostEstimate(
                flops=10 * group * tokens * tree_dev * tokens * head_dim,
                bytes_accessed=8 * 1024 * 1024,
                transcendentals=group * tokens * tree_dev * tokens,
            ),
            name="attend",
        )(plan, k_gain_row, *tables, *pieces[h], *queries[5 * h:5 * h + 5])

    dq, attended, k_gain_parts = [], [], []
    for h in range(kv_heads):
        dq_here, k_gain_part, *parts, crossed_part = attend(h)
        dq.append(dq_here)
        k_gain_parts.append(k_gain_part)
        attended.append((parts, crossed_part))

    everyone = cycle * lax.axis_size("heads")
    dq_raw, gains = pl.pallas_call(
        lambda *refs: query_kernel(blocks, inv_root, kv_heads, *refs),
        out_shape=(sds((tokens, heads * head_dim), BF16), sds((everyone, 2, head_dim), F32)),
        in_specs=[smem] + [vmem] * (6 + 2 * kv_heads),
        out_specs=(vmem, vmem),
        compiler_params=params,
        name="query_back",
    )(depth, *tables, q_gain_row, q_raw, *dq, *k_gain_parts)

    terms, farthest = [], []
    for h, (parts, crossed_part) in enumerate(attended):
        if h < kv_heads - 1:
            others = tree.across(crossed_part, [0, *steps], back=True)
            merged = [
                (parts[i + 1].astype(F32) + others[i + 1].astype(F32)).astype(BF16) for i in range(len(steps))
            ]
            farthest.append(merged.pop())
        else:
            others = tree.across(crossed_part, steps, back=True)
            *merged, near, joined, gains = pl.pallas_call(
                merge_kernel,
                out_shape=(
                    *[sds((tokens, 2 * head_dim), BF16)] * len(steps),
                    sds((kv_heads, tokens, 2 * head_dim), BF16),
                    sds(gains.shape, F32),
                ),
                in_specs=[vmem] * (len(steps) + 4),
                out_specs=tuple([vmem] * (len(steps) + 2)),
                compiler_params=params,
                name="merge",
            )(*parts[1:], others, gains, jnp.stack(farthest))
            joined = tree.home(joined, steps[-1])
            others = tree.across(near[None], [0], back=True)
        mine = [(parts[0], None), (others, 0)]
        terms.append(mine + [(tree.home(both, step), None) for both, step in zip(merged, steps)])
    for h in range(kv_heads):
        if h < kv_heads - 1:
            arrays, places = zip(*terms[h])
            early, gains = pl.pallas_call(
                lambda *refs: early_kernel(places, *refs),
                out_shape=(sds((tokens, 2 * head_dim), F32), sds(gains.shape, F32)),
                in_specs=[vmem] * (1 + len(arrays)),
                out_specs=(vmem, vmem),
                compiler_params=params,
                cost_estimate=slow,
                name="early",
            )(gains, *arrays)
            terms[h] = [(early, None)]
        terms[h].append((joined, h))
    gains = lax.all_to_all(gains, ("ctx", "heads"), 0, 0)

    arrays = [array for mine in terms for array, _ in mine]
    places = [[place for _, place in mine] for mine in terms]
    dk_raw, dv, total = pl.pallas_call(
        lambda *refs: key_kernel(blocks, places, *refs),
        out_shape=(sds(k_raw.shape, BF16), sds(k_raw.shape, BF16), sds(gains.shape[1:], F32)),
        in_specs=[smem] + [vmem] * (7 + len(arrays)),
        out_specs=(vmem, vmem, vmem),
        compiler_params=params,
        name="key_back",
    )(depth, *tables, k_gain_row, k_raw, gains, *arrays)
    return (dq_raw, dk_raw, dv, total[0], total[1])


def solution(mesh):
    split = P("ctx", "heads")
    return jax.shard_map(
        on_device,
        mesh=mesh,
        in_specs=(split, split, split, split, split, P(), P(), P("ctx", None)),
        out_specs=(split, split, split, P(), P()),
        check_vma=False,
    )
```

profile of v0, /device:TPU:0, one launch (start us, length us, event | category | flops | bytes accessed | tf_op | source)
XLA Modules:
  0.0 108.6 jit_solution(11941050735665819477)
XLA Ops:
  0.6 1.0 fusion.7
  1.7 1.3 %collective-permute-start = (bf16[256,256]{1,0:T(8,128)(2,1)S(1)}, bf16[256,256]{1,0:T(8,128)(2,1)S(1)}, u32[]{:S(2)}, u32[]{:S(2)}) collective-permute-start(bf16[256,256]{1,0:T(8,128)(2,1)S(1)} %pad_maximum_fusion.refs_6_), channel_id=1, source_target_pairs={{4,12},{8,16},{12,20},{16,24},{20,28},{24,0},{28,4},{5,13},{9,17},... | collective-permute-start | bytes 393224 | tf_op jit(solution)/shard_map/ppermute | solution.py:357
  3.0 1.3 %collective-permute-start.1 = (bf16[256,256]{1,0:T(8,128)(2,1)S(1)}, bf16[256,256]{1,0:T(8,128)(2,1)S(1)}, u32[]{:S(2)}, u32[]{:S(2)}) collective-permute-start(bf16[256,256]{1,0:T(8,128)(2,1)S(1)} %pad_maximum_fusion.refs_6_), channel_id=1, source_target_pairs={{4,20},{8,24},{12,28},{16,0},{20,4},{5,21},{9,25},{13,29},{17,1},{... | collective-permute-start | bytes 393224 | tf_op jit(solution)/shard_map/ppermute | solution.py:357
  4.3 1.3 %collective-permute-start.2 = (bf16[256,256]{1,0:T(8,128)(2,1)S(1)}, bf16[256,256]{1,0:T(8,128)(2,1)S(1)}, u32[]{:S(2)}, u32[]{:S(2)}) collective-permute-start(bf16[256,256]{1,0:T(8,128)(2,1)S(1)} %pad_maximum_fusion.refs_6_), channel_id=1, source_target_pairs={{4,28},{8,0},{12,4},{5,29},{9,1},{13,5},{6,30},{10,2},{14,6},{7,31... | collective-permute-start | bytes 393224 | tf_op jit(solution)/shard_map/ppermute | solution.py:357
  5.6 1.3 %collective-permute-start.3 = (bf16[256,256]{1,0:T(8,128)(2,1)S(1)}, bf16[256,256]{1,0:T(8,128)(2,1)S(1)}, u32[]{:S(2)}, u32[]{:S(2)}) collective-permute-start(bf16[256,256]{1,0:T(8,128)(2,1)S(1)} %pad_maximum_fusion.refs_6_), channel_id=1, source_target_pairs={{4,0},{8,12},{16,20},{24,28},{5,1},{9,13},{17,21},{25,29},{6,2},{1... | collective-permute-start | bytes 393224 | tf_op jit(solution)/shard_map/ppermute | solution.py:357
  6.9 1.3 %collective-permute-start.5 = (bf16[256,256]{1,0:T(8,128)(2,1)S(1)}, bf16[256,256]{1,0:T(8,128)(2,1)S(1)}, u32[]{:S(2)}, u32[]{:S(2)}) collective-permute-start(bf16[256,256]{1,0:T(8,128)(2,1)S(1)} %pad_maximum_fusion.1.refs_0_.refs_6_), channel_id=1, source_target_pairs={{4,12},{8,16},{12,20},{16,24},{20,28},{24,0},{28,4},{5,13},{9,17},... | collective-permute-start | bytes 393224 | tf_op jit(solution)/shard_map/ppermute | solution.py:357
  8.3 0.0 copy-start.12
  8.3 0.7 copy-done.12
  8.9 0.7 fusion.6
  9.7 2.0 %plan.1.refs_4_.refs_0_ = s32[5,32]{1,0:T(8,128)} custom-call(s32[1]{0:T(128)} %bitcast.1.refs_0_, s32[4,32]{1,0:T(4,128)} %get-tuple-element.86.refs_1_), custom_call_target="tpu_custom_call" | custom-call | flops 1024 | bytes 1024 | tf_op jit(solution)/shard_map/plan/pallas_call | solution.py:420
  11.7 0.0 copy-start.2
  11.7 0.0 copy-start.3
  11.7 0.0 copy-start.4
  11.7 0.0 copy-start.5
  11.7 0.5 collective-permute-done.refs_0_.refs_7_
  12.3 1.3 %collective-permute-start.6 = (bf16[256,256]{1,0:T(8,128)(2,1)S(1)}, bf16[256,256]{1,0:T(8,128)(2,1)S(1)}, u32[]{:S(2)}, u32[]{:S(2)}) collective-permute-start(bf16[256,256]{1,0:T(8,128)(2,1)S(1)} %pad_maximum_fusion.1.refs_0_.refs_6_), channel_id=1, source_target_pairs={{4,20},{8,24},{12,28},{16,0},{20,4},{5,21},{9,25},{13,29},{17,1},{... | collective-permute-start | bytes 393224 | tf_op jit(solution)/shard_map/ppermute | solution.py:357
  13.5 1.5 %collective-permute-done.1.refs_1_.refs_8_ = bf16[256,256]{1,0:T(8,128)(2,1)S(1)} collective-permute-done((bf16[256,256]{1,0:T(8,128)(2,1)S(1)}, bf16[256,256]{1,0:T(8,128)(2,1)S(1)}, u32[]{:S(2)}, u32[]{:S(2)}) %collective-permute-start.1) | collective-permute-done | bytes 131104 | tf_op jit(solution)/shard_map/ppermute | solution.py:357
  15.1 1.3 %collective-permute-start.7 = (bf16[256,256]{1,0:T(8,128)(2,1)S(1)}, bf16[256,256]{1,0:T(8,128)(2,1)S(1)}, u32[]{:S(2)}, u32[]{:S(2)}) collective-permute-start(bf16[256,256]{1,0:T(8,128)(2,1)S(1)} %pad_maximum_fusion.1.refs_0_.refs_6_), channel_id=1, source_target_pairs={{4,28},{8,0},{12,4},{5,29},{9,1},{13,5},{6,30},{10,2},{14,6},{7,31... | collective-permute-start | bytes 393224 | tf_op jit(solution)/shard_map/ppermute | solution.py:357
  16.4 4.2 %collective-permute-done.2.refs_2_.refs_9_ = bf16[256,256]{1,0:T(8,128)(2,1)S(1)} collective-permute-done((bf16[256,256]{1,0:T(8,128)(2,1)S(1)}, bf16[256,256]{1,0:T(8,128)(2,1)S(1)}, u32[]{:S(2)}, u32[]{:S(2)}) %collective-permute-start.2) | collective-permute-done | bytes 131104 | tf_op jit(solution)/shard_map/ppermute | solution.py:357
  20.6 0.7 copy-done.6
  21.3 0.0 copy-start.8
  21.3 1.3 %collective-permute-start.4 = (bf16[3,256,256]{2,1,0:T(8,128)(2,1)S(1)}, bf16[3,256,256]{2,1,0:T(8,128)(2,1)S(1)}, u32[]{:S(2)}, u32[]{:S(2)}) collective-permute-start(bf16[3,256,256]{2,1,0:T(8,128)(2,1)S(1)} %join.2), channel_id=1, source_target_pairs={{4,0},{12,8},{16,20},{20,16},{24,28},{28,24},{5,1},{13,9},{17,21},... | collective-permute-start | bytes 1179656 | tf_op jit(solution)/shard_map/ppermute | solution.py:357
  22.7 0.0 copy-start.10
  22.7 1.2 %copy-done.10 = bf16[256,2048]{1,0:T(8,128)(2,1)S(1)} copy-done((bf16[256,2048]{1,0:T(8,128)(2,1)S(1)}, bf16[256,2048]{1,0:T(8,128)(2,1)}, u32[]{:S(2)}) %copy-start.10) | copy-done | bytes 1048600
  23.9 1.2 %copy-done.11 = bf16[256,2048]{1,0:T(8,128)(2,1)S(1)} copy-done((bf16[256,2048]{1,0:T(8,128)(2,1)S(1)}, bf16[256,2048]{1,0:T(8,128)(2,1)}, u32[]{:S(2)}) %copy-start.11) | copy-done | bytes 1048600
  25.1 4.1 %prep.1 = (bf16[128,2048]{1,0:T(8,128)(2,1)S(1)}, bf16[2048,128]{1,0:T(8,128)(2,1)S(1)}, bf16[128,2048]{1,0:T(8,128)(2,1)S(1)}, bf16[2048,128]{1,0:T(8,128)(2,1)...) custom-call(s32[4]{0:T(128)S(1)} %broadcast_add_fusion.refs_0_, ...), custom_call_target="tpu_custom_call" | custom-call | flops 4000000000 | bytes 16777216 | tf_op jit(solution)/shard_map/prep/pallas_call | solution.py:442
  29.3 1.3 %collective-permute-start.8 = (bf16[4,256,256]{2,1,0:T(8,128)(2,1)S(1)}, bf16[4,256,256]{2,1,0:T(8,128)(2,1)S(1)}, u32[]{:S(2)}, u32[]{:S(2)}) collective-permute-start(bf16[4,256,256]{2,1,0:T(8,128)(2,1)S(1)} %join.3), channel_id=1, source_target_pairs={{4,0},{8,12},{12,8},{16,20},{20,16},{24,28},{28,24},{5,1},{9,13},{... | collective-permute-start | bytes 1572872 | tf_op jit(solution)/shard_map/ppermute | solution.py:357
  30.6 8.2 %collective-permute-done.4.refs_11_ = bf16[3,256,256]{2,1,0:T(8,128)(2,1)S(1)} collective-permute-done((bf16[3,256,256]{2,1,0:T(8,128)(2,1)S(1)}, bf16[3,256,256]{2,1,0:T(8,128)(2,1)S(1)}, u32[]{:S(2)}, u32[]{:S(2)}) %collective-permute-start.4) | collective-permute-done | bytes 393248 | tf_op jit(solution)/shard_map/ppermute | solution.py:357
  38.8 0.7 copy-done.7
  39.5 16.3 %attend.2 = (f32[128,2048]{1,0:T(8,128)S(1)}, f32[8,128]{1,0:T(8,128)S(1)}, bf16[256,256]{1,0:T(8,128)(2,1)S(1)}, bf16[256,256]{1,0:T(8,128)(2,1)S(1)}, bf16[256...) custom-call(s32[5,32]{1,0:T(8,128)S(1)} %copy-done.7, f32[1,128]{1,0:T(1,128)S(1)} %bitcast.27, ...), custom_call_target="tpu_custom_call" | custom-call | flops 5368709120 | bytes 8388608 | tf_op jit(solution)/shard_map/attend/pallas_call | solution.py:476
  55.8 1.5 %collective-permute-start.10 = (bf16[4,256,256]{2,1,0:T(8,128)(2,1)S(1)}, bf16[4,256,256]{2,1,0:T(8,128)(2,1)S(1)}, u32[]{:S(2)}, u32[]{:S(2)}) collective-permute-start(bf16[4,256,256]{2,1,0:T(8,128)(2,1)S(1)} %get-tuple-element.64), channel_id=1, source_target_pairs={{0,4},{8,12},{12,8},{16,20},{20,16},{24,28},{28,24},{1,5},{9,13},{... | collective-permute-start | bytes 1572872 | tf_op jit(solution)/shard_map/ppermute | solution.py:357
  57.3 16.3 %attend.3 = (f32[128,2048]{1,0:T(8,128)S(1)}, f32[8,128]{1,0:T(8,128)S(1)}, bf16[256,256]{1,0:T(8,128)(2,1)S(1)}, bf16[256,256]{1,0:T(8,128)(2,1)S(1)}, bf16[256...) custom-call(s32[5,32]{1,0:T(8,128)S(1)} %copy-done.7, ...), custom_call_target="tpu_custom_call" | custom-call | flops 5368709120 | bytes 8388608 | tf_op jit(solution)/shard_map/attend/pallas_call | solution.py:476
  73.6 1.3 %collective-permute-start.9 = (bf16[3,256,256]{2,1,0:T(8,128)(2,1)S(1)}, bf16[3,256,256]{2,1,0:T(8,128)(2,1)S(1)}, u32[]{:S(2)}, u32[]{:S(2)}) collective-permute-start(bf16[3,256,256]{2,1,0:T(8,128)(2,1)S(1)} %get-tuple-element.61), channel_id=1, source_target_pairs={{0,4},{8,12},{16,20},{20,16},{24,28},{28,24},{1,5},{9,13},{17,21},... | collective-permute-start | bytes 1179656 | tf_op jit(solution)/shard_map/ppermute | solution.py:357
  74.9 0.1 fusion
  75.0 1.8 %collective-permute-start.11 = (bf16[256,256]{1,0:T(8,128)(2,1)S(1)}, bf16[256,256]{1,0:T(8,128)(2,1)S(1)}, u32[]{:S(2)}, u32[]{:S(2)}) collective-permute-start(bf16[256,256]{1,0:T(8,128)(2,1)S(1)} %get-tuple-element.80), channel_id=1, source_target_pairs={{0,24},{4,28},{12,4},{16,8},{20,12},{24,16},{28,20},{1,25},{5,29},... | collective-permute-start | bytes 393224 | tf_op jit(solution)/shard_map/ppermute | solution.py:357
  76.9 1.3 %collective-permute-start.12 = (bf16[256,256]{1,0:T(8,128)(2,1)S(1)}, bf16[256,256]{1,0:T(8,128)(2,1)S(1)}, u32[]{:S(2)}, u32[]{:S(2)}) collective-permute-start(bf16[256,256]{1,0:T(8,128)(2,1)S(1)} %get-tuple-element.79), channel_id=1, source_target_pairs={{0,16},{4,20},{20,4},{24,8},{28,12},{1,17},{5,21},{21,5},{25,9},{2... | collective-permute-start | bytes 393224 | tf_op jit(solution)/shard_map/ppermute | solution.py:357
  78.2 4.6 %query_back.1 = (bf16[256,2048]{1,0:T(8,128)(2,1)}, f32[32,2,128]{2,1,0:T(2,128)S(1)}) custom-call(s32[4]{0:T(128)S(1)} %broadcast_add_fusion.refs_0_, f32[32,128]{1,0:T(8,128)S(1)} %copy-done.4, f32[32,128]{1,0:T(8,128)S(1)} %copy-done.5, f32[64,128]{1,0:T(8,128)S(1)} %copy-done.2, f32[64,128]{1,0:T(8,128)S(1)} %copy-done.3, f32[1,128]{1,0:T(1,128)S(1)} %bitcast.26, ...), custom_call_target="tpu_custom_call" | custom-call | tf_op jit(solution)/shard_map/query_back/pallas_call | solution.py:517
  82.8 0.1 merge.1
  82.9 1.3 %collective-permute-start.13 = (bf16[2,256,256]{2,1,0:T(8,128)(2,1)S(1)}, bf16[2,256,256]{2,1,0:T(8,128)(2,1)S(1)}, u32[]{:S(2)}, u32[]{:S(2)}) collective-permute-start(bf16[2,256,256]{2,1,0:T(8,128)(2,1)S(1)} %get-tuple-element.71), channel_id=1, source_target_pairs={{0,8},{4,12},{28,4},{1,9},{5,13},{29,5},{2,10},{6,14},{30,6},{3,11... | collective-permute-start | bytes 786440 | tf_op jit(solution)/shard_map/ppermute | solution.py:357
  84.2 3.6 %collective-permute-start.14 = (bf16[1,256,256]{2,1,0:T(8,128)(2,1)S(1)}, bf16[1,256,256]{2,1,0:T(8,128)(2,1)S(1)}, u32[]{:S(2)}, u32[]{:S(2)}) collective-permute-start(bf16[1,256,256]{2,1,0:T(8,128)(2,1)S(1)} %bitcast.30), channel_id=1, source_target_pairs={{0,4},{12,8},{20,16},{28,24},{1,5},{13,9},{21,17},{29,25},{2,6},{1... | collective-permute-start | bytes 393224 | tf_op jit(solution)/shard_map/ppermute | solution.py:357
  87.8 1.3 %collective-permute-start.15 = (bf16[256,256]{1,0:T(8,128)(2,1)S(1)}, bf16[256,256]{1,0:T(8,128)(2,1)S(1)}, u32[]{:S(2)}, u32[]{:S(2)}) collective-permute-start(bf16[256,256]{1,0:T(8,128)(2,1)S(1)} %get-tuple-element.74), channel_id=1, source_target_pairs={{0,24},{4,28},{12,4},{16,8},{20,12},{24,16},{28,20},{1,25},{5,29},... | collective-permute-start | bytes 393224 | tf_op jit(solution)/shard_map/ppermute | solution.py:357
  89.1 1.3 %collective-permute-start.16 = (bf16[256,256]{1,0:T(8,128)(2,1)S(1)}, bf16[256,256]{1,0:T(8,128)(2,1)S(1)}, u32[]{:S(2)}, u32[]{:S(2)}) collective-permute-start(bf16[256,256]{1,0:T(8,128)(2,1)S(1)} %get-tuple-element.75), channel_id=1, source_target_pairs={{0,16},{4,20},{20,4},{24,8},{28,12},{1,17},{5,21},{21,5},{25,9},{2... | collective-permute-start | bytes 393224 | tf_op jit(solution)/shard_map/ppermute | solution.py:357
  90.5 0.0 copy-start.1
  90.5 0.6 early.1
  91.1 8.1 %all-to-all-start = ((f32[32,2,128]{2,1,0:T(2,128)}), f32[32,2,128]{2,1,0:T(2,128)S(1)}, u32[]{:S(2)}, u32[]{:S(2)}) async-start(f32[32,2,128]{2,1,0:T(2,128)} %get-tuple-element.69), calls=%async_computation | async-start | bytes 65536 | tf_op jit(solution)/shard_map/all_to_all | solution.py:566
  99.3 7.2 %all-to-all-done.refs_7_ = f32[32,2,128]{2,1,0:T(2,128)S(1)} async-done(((f32[32,2,128]{2,1,0:T(2,128)}), f32[32,2,128]{2,1,0:T(2,128)S(1)}, u32[]{:S(2)}, u32[]{:S(2)}) %all-to-all-start) | async-done | bytes 32800 | tf_op jit(solution)/shard_map/all_to_all | solution.py:566
  106.5 1.6 %key_back.1 = (bf16[256,256]{1,0:T(8,128)(2,1)}, bf16[256,256]{1,0:T(8,128)(2,1)}, f32[2,128]{1,0:T(2,128)S(1)}) custom-call(s32[4]{0:T(128)S(1)} %broadcast_add_fusion.refs_0_, f32[32,128]{1,0:T(8,128)S(1)} %copy-done.4, f32[32,128]{1,0:T(8,128)S(1)} %copy-done.5, f32[64,128]{1,0:T(8,128)S(1)} %copy-done.2, f32[64,128]{1,0:T(8,128)S(1)} %copy-done.3, ...), custom_call_target="tpu_custom_call" | custom-call | tf_op jit(solution)/shard_map/key_back/pallas_call | solution.py:570
  108.1 0.5 slice_bitcast_fusion.3
  (31 shorter events, 0.2 us)
Async XLA Ops:
  0.6 22.0 %copy-start = (bf16[256,2048]{1,0:T(8,128)(2,1)S(1)}, bf16[256,2048]{1,0:T(8,128)(2,1)}, u32[]{:S(2)}) copy-start(bf16[256,2048]{1,0:T(8,128)(2,1)} %refs_6_.4) | copy-start | bytes 3145732
  1.7 10.5 %collective-permute-start = (bf16[256,256]{1,0:T(8,128)(2,1)S(1)}, bf16[256,256]{1,0:T(8,128)(2,1)S(1)}, u32[]{:S(2)}, u32[]{:S(2)}) collective-permute-start(bf16[256,256]{1,0:T(8,128)(2,1)S(1)} %pad_maximum_fusion.refs_6_), channel_id=1, source_target_pairs={{4,12},{8,16},{12,20},{16,24},{20,28},{24,0},{28,4},{5,13},{9,17},... | collective-permute-start | bytes 393224 | tf_op jit(solution)/shard_map/ppermute | solution.py:357
  3.0 12.1 %collective-permute-start.1 = (bf16[256,256]{1,0:T(8,128)(2,1)S(1)}, bf16[256,256]{1,0:T(8,128)(2,1)S(1)}, u32[]{:S(2)}, u32[]{:S(2)}) collective-permute-start(bf16[256,256]{1,0:T(8,128)(2,1)S(1)} %pad_maximum_fusion.refs_6_), channel_id=1, source_target_pairs={{4,20},{8,24},{12,28},{16,0},{20,4},{5,21},{9,25},{13,29},{17,1},{... | collective-permute-start | bytes 393224 | tf_op jit(solution)/shard_map/ppermute | solution.py:357
  4.3 16.3 %collective-permute-start.2 = (bf16[256,256]{1,0:T(8,128)(2,1)S(1)}, bf16[256,256]{1,0:T(8,128)(2,1)S(1)}, u32[]{:S(2)}, u32[]{:S(2)}) collective-permute-start(bf16[256,256]{1,0:T(8,128)(2,1)S(1)} %pad_maximum_fusion.refs_6_), channel_id=1, source_target_pairs={{4,28},{8,0},{12,4},{5,29},{9,1},{13,5},{6,30},{10,2},{14,6},{7,31... | collective-permute-start | bytes 393224 | tf_op jit(solution)/shard_map/ppermute | solution.py:357
  5.6 15.0 %collective-permute-start.3 = (bf16[256,256]{1,0:T(8,128)(2,1)S(1)}, bf16[256,256]{1,0:T(8,128)(2,1)S(1)}, u32[]{:S(2)}, u32[]{:S(2)}) collective-permute-start(bf16[256,256]{1,0:T(8,128)(2,1)S(1)} %pad_maximum_fusion.refs_6_), channel_id=1, source_target_pairs={{4,0},{8,12},{16,20},{24,28},{5,1},{9,13},{17,21},{25,29},{6,2},{1... | collective-permute-start | bytes 393224 | tf_op jit(solution)/shard_map/ppermute | solution.py:357
  6.9 22.3 %collective-permute-start.5 = (bf16[256,256]{1,0:T(8,128)(2,1)S(1)}, bf16[256,256]{1,0:T(8,128)(2,1)S(1)}, u32[]{:S(2)}, u32[]{:S(2)}) collective-permute-start(bf16[256,256]{1,0:T(8,128)(2,1)S(1)} %pad_maximum_fusion.1.refs_0_.refs_6_), channel_id=1, source_target_pairs={{4,12},{8,16},{12,20},{16,24},{20,28},{24,0},{28,4},{5,13},{9,17},... | collective-permute-start | bytes 393224 | tf_op jit(solution)/shard_map/ppermute | solution.py:357
  8.3 0.7 copy-start.12
  11.7 11.0 %copy-start.2 = (f32[64,128]{1,0:T(8,128)S(1)}, f32[64,128]{1,0:T(8,128)}, u32[]{:S(2)}) copy-start(f32[64,128]{1,0:T(8,128)} %constant.66.clone.refs_3_.refs_4_) | copy-start | bytes 98308
  11.7 10.9 %copy-start.3 = (f32[64,128]{1,0:T(8,128)S(1)}, f32[64,128]{1,0:T(8,128)}, u32[]{:S(2)}) copy-start(f32[64,128]{1,0:T(8,128)} %constant.67.clone.refs_4_.refs_5_) | copy-start | bytes 98308
  11.7 10.9 %copy-start.4 = (f32[32,128]{1,0:T(8,128)S(1)}, f32[32,128]{1,0:T(8,128)}, u32[]{:S(2)}) copy-start(f32[32,128]{1,0:T(8,128)} %constant.64.clone.refs_1_.refs_2_) | copy-start | bytes 49156
  11.7 10.9 %copy-start.5 = (f32[32,128]{1,0:T(8,128)S(1)}, f32[32,128]{1,0:T(8,128)}, u32[]{:S(2)}) copy-start(f32[32,128]{1,0:T(8,128)} %constant.65.clone.refs_2_.refs_3_) | copy-start | bytes 49156
  12.3 17.0 %collective-permute-start.6 = (bf16[256,256]{1,0:T(8,128)(2,1)S(1)}, bf16[256,256]{1,0:T(8,128)(2,1)S(1)}, u32[]{:S(2)}, u32[]{:S(2)}) collective-permute-start(bf16[256,256]{1,0:T(8,128)(2,1)S(1)} %pad_maximum_fusion.1.refs_0_.refs_6_), channel_id=1, source_target_pairs={{4,20},{8,24},{12,28},{16,0},{20,4},{5,21},{9,25},{13,29},{17,1},{... | collective-permute-start | bytes 393224 | tf_op jit(solution)/shard_map/ppermute | solution.py:357
  15.1 14.2 %collective-permute-start.7 = (bf16[256,256]{1,0:T(8,128)(2,1)S(1)}, bf16[256,256]{1,0:T(8,128)(2,1)S(1)}, u32[]{:S(2)}, u32[]{:S(2)}) collective-permute-start(bf16[256,256]{1,0:T(8,128)(2,1)S(1)} %pad_maximum_fusion.1.refs_0_.refs_6_), channel_id=1, source_target_pairs={{4,28},{8,0},{12,4},{5,29},{9,1},{13,5},{6,30},{10,2},{14,6},{7,31... | collective-permute-start | bytes 393224 | tf_op jit(solution)/shard_map/ppermute | solution.py:357
  20.6 0.7 copy-start.6
  21.3 1.4 %copy-start.8 = (f32[128]{0:T(128)S(1)}, f32[128]{0:T(128)}, u32[]{:S(2)}) copy-start(f32[128]{0:T(128)} %param.17) | copy-start | bytes 1540
  21.3 17.4 %collective-permute-start.4 = (bf16[3,256,256]{2,1,0:T(8,128)(2,1)S(1)}, bf16[3,256,256]{2,1,0:T(8,128)(2,1)S(1)}, u32[]{:S(2)}, u32[]{:S(2)}) collective-permute-start(bf16[3,256,256]{2,1,0:T(8,128)(2,1)S(1)} %join.2), channel_id=1, source_target_pairs={{4,0},{12,8},{16,20},{20,16},{24,28},{28,24},{5,1},{13,9},{17,21},... | collective-permute-start | bytes 1179656 | tf_op jit(solution)/shard_map/ppermute | solution.py:357
  22.7 1.2 %copy-start.10 = (bf16[256,2048]{1,0:T(8,128)(2,1)S(1)}, bf16[256,2048]{1,0:T(8,128)(2,1)}, u32[]{:S(2)}) copy-start(bf16[256,2048]{1,0:T(8,128)(2,1)} %refs_7_.1) | copy-start | bytes 3145732
  23.9 1.2 %copy-start.11 = (bf16[256,2048]{1,0:T(8,128)(2,1)S(1)}, bf16[256,2048]{1,0:T(8,128)(2,1)}, u32[]{:S(2)}) copy-start(bf16[256,2048]{1,0:T(8,128)(2,1)} %refs_8_.1) | copy-start | bytes 3145732
  29.3 28.0 %collective-permute-start.8 = (bf16[4,256,256]{2,1,0:T(8,128)(2,1)S(1)}, bf16[4,256,256]{2,1,0:T(8,128)(2,1)S(1)}, u32[]{:S(2)}, u32[]{:S(2)}) collective-permute-start(bf16[4,256,256]{2,1,0:T(8,128)(2,1)S(1)} %join.3), channel_id=1, source_target_pairs={{4,0},{8,12},{12,8},{16,20},{20,16},{24,28},{28,24},{5,1},{9,13},{... | collective-permute-start | bytes 1572872 | tf_op jit(solution)/shard_map/ppermute | solution.py:357
  38.8 0.7 copy-start.7
  38.8 0.7 copy-start.9
  55.8 19.2 %collective-permute-start.10 = (bf16[4,256,256]{2,1,0:T(8,128)(2,1)S(1)}, bf16[4,256,256]{2,1,0:T(8,128)(2,1)S(1)}, u32[]{:S(2)}, u32[]{:S(2)}) collective-permute-start(bf16[4,256,256]{2,1,0:T(8,128)(2,1)S(1)} %get-tuple-element.64), channel_id=1, source_target_pairs={{0,4},{8,12},{12,8},{16,20},{20,16},{24,28},{28,24},{1,5},{9,13},{... | collective-permute-start | bytes 1572872 | tf_op jit(solution)/shard_map/ppermute | solution.py:357
  73.6 9.2 %collective-permute-start.9 = (bf16[3,256,256]{2,1,0:T(8,128)(2,1)S(1)}, bf16[3,256,256]{2,1,0:T(8,128)(2,1)S(1)}, u32[]{:S(2)}, u32[]{:S(2)}) collective-permute-start(bf16[3,256,256]{2,1,0:T(8,128)(2,1)S(1)} %get-tuple-element.61), channel_id=1, source_target_pairs={{0,4},{8,12},{16,20},{20,16},{24,28},{28,24},{1,5},{9,13},{17,21},... | collective-permute-start | bytes 1179656 | tf_op jit(solution)/shard_map/ppermute | solution.py:357
  75.0 14.1 %collective-permute-start.11 = (bf16[256,256]{1,0:T(8,128)(2,1)S(1)}, bf16[256,256]{1,0:T(8,128)(2,1)S(1)}, u32[]{:S(2)}, u32[]{:S(2)}) collective-permute-start(bf16[256,256]{1,0:T(8,128)(2,1)S(1)} %get-tuple-element.80), channel_id=1, source_target_pairs={{0,24},{4,28},{12,4},{16,8},{20,12},{24,16},{28,20},{1,25},{5,29},... | collective-permute-start | bytes 393224 | tf_op jit(solution)/shard_map/ppermute | solution.py:357
  76.9 13.6 %collective-permute-start.12 = (bf16[256,256]{1,0:T(8,128)(2,1)S(1)}, bf16[256,256]{1,0:T(8,128)(2,1)S(1)}, u32[]{:S(2)}, u32[]{:S(2)}) collective-permute-start(bf16[256,256]{1,0:T(8,128)(2,1)S(1)} %get-tuple-element.79), channel_id=1, source_target_pairs={{0,16},{4,20},{20,4},{24,8},{28,12},{1,17},{5,21},{21,5},{25,9},{2... | collective-permute-start | bytes 393224 | tf_op jit(solution)/shard_map/ppermute | solution.py:357
  82.9 23.6 %collective-permute-start.13 = (bf16[2,256,256]{2,1,0:T(8,128)(2,1)S(1)}, bf16[2,256,256]{2,1,0:T(8,128)(2,1)S(1)}, u32[]{:S(2)}, u32[]{:S(2)}) collective-permute-start(bf16[2,256,256]{2,1,0:T(8,128)(2,1)S(1)} %get-tuple-element.71), channel_id=1, source_target_pairs={{0,8},{4,12},{28,4},{1,9},{5,13},{29,5},{2,10},{6,14},{30,6},{3,11... | collective-permute-start | bytes 786440 | tf_op jit(solution)/shard_map/ppermute | solution.py:357
  84.2 15.0 %collective-permute-start.14 = (bf16[1,256,256]{2,1,0:T(8,128)(2,1)S(1)}, bf16[1,256,256]{2,1,0:T(8,128)(2,1)S(1)}, u32[]{:S(2)}, u32[]{:S(2)}) collective-permute-start(bf16[1,256,256]{2,1,0:T(8,128)(2,1)S(1)} %bitcast.30), channel_id=1, source_target_pairs={{0,4},{12,8},{20,16},{28,24},{1,5},{13,9},{21,17},{29,25},{2,6},{1... | collective-permute-start | bytes 393224 | tf_op jit(solution)/shard_map/ppermute | solution.py:357
  87.8 11.4 %collective-permute-start.15 = (bf16[256,256]{1,0:T(8,128)(2,1)S(1)}, bf16[256,256]{1,0:T(8,128)(2,1)S(1)}, u32[]{:S(2)}, u32[]{:S(2)}) collective-permute-start(bf16[256,256]{1,0:T(8,128)(2,1)S(1)} %get-tuple-element.74), channel_id=1, source_target_pairs={{0,24},{4,28},{12,4},{16,8},{20,12},{24,16},{28,20},{1,25},{5,29},... | collective-permute-start | bytes 393224 | tf_op jit(solution)/shard_map/ppermute | solution.py:357
  89.1 10.1 %collective-permute-start.16 = (bf16[256,256]{1,0:T(8,128)(2,1)S(1)}, bf16[256,256]{1,0:T(8,128)(2,1)S(1)}, u32[]{:S(2)}, u32[]{:S(2)}) collective-permute-start(bf16[256,256]{1,0:T(8,128)(2,1)S(1)} %get-tuple-element.75), channel_id=1, source_target_pairs={{0,16},{4,20},{20,4},{24,8},{28,12},{1,17},{5,21},{21,5},{25,9},{2... | collective-permute-start | bytes 393224 | tf_op jit(solution)/shard_map/ppermute | solution.py:357
  90.5 16.0 %copy-start.1 = (bf16[256,256]{1,0:T(8,128)(2,1)S(1)}, bf16[256,256]{1,0:T(8,128)(2,1)}, u32[]{:S(2)}) copy-start(bf16[256,256]{1,0:T(8,128)(2,1)} %refs_6_.5) | copy-start | bytes 393220
  91.1 15.4 %all-to-all-start = ((f32[32,2,128]{2,1,0:T(2,128)}), f32[32,2,128]{2,1,0:T(2,128)S(1)}, u32[]{:S(2)}, u32[]{:S(2)}) async-start(f32[32,2,128]{2,1,0:T(2,128)} %get-tuple-element.69), calls=%async_computation | async-start | bytes 65536 | tf_op jit(solution)/shard_map/all_to_all | solution.py:566
where the time goes:
time: 109 us
  Pallas kernels  45.7 us (42%)
  starting transfers between devices  33.2 us (30%)
  waiting for transfers between devices  21.7 us (20%)
  local copies, waits for them, and re-layouts  6.1 us (6%)
    pallas_call x2, Pallas kernels, attend(): pl.pallas_call(lambda *refs: main_kernel(blocks, block_len, tree_dev, inv...  32.6 us
    ppermute x17, starting transfers between devices, send(): return lax.ppermute(value, 'ctx', pairs)  25.1 us
    ppermute x17, waiting for transfers between devices, send(): return lax.ppermute(value, 'ctx', pairs)  14.5 us
    all_to_all x1, starting transfers between devices, on_device(): gains = lax.all_to_all(gains, ('ctx', 'heads'), 0, 0)  8.11 us
    all_to_all x1, waiting for transfers between devices, on_device(): gains = lax.all_to_all(gains, ('ctx', 'heads'), 0, 0)  7.22 us
    pallas_call x1, Pallas kernels, on_device(): pl.pallas_call(lambda *refs: query_kernel(blocks, inv_root, kv_heads, *re...  4.6 us
    unnamed x26, local copies, waits for them, and re-layouts  4.54 us
    pallas_call x1, Pallas kernels, on_device(): pl.pallas_call(lambda *refs: prep_kernel(blocks, block_len, kv_heads, *re...  4.08 us
  transfers between devices with their start and end apart: 18, of which 5 were waited for; matrix products, arithmetic and copies ran while one was open for 1% of the time, Pallas kernels for 41%

commit v1 on v0

--- a/solution.py
+++ b/solution.py
@@ -318,7 +318,7 @@
 def early_kernel(places, gains_ref, *refs):
     terms, (sum_ref, gains_out_ref) = refs[:-2], refs[-2:]
     sum_ref[...] = summed_terms(terms, places)
-    gains_out_ref[...] = gains_ref[...]
+    gains_out_ref[...] = jnp.broadcast_to(jnp.sum(gains_ref[...], 0, keepdims=True), gains_out_ref.shape)
 
 
 def key_kernel(blocks, places, depth_ref, t0, t1, t2, t3, gain_ref, k_ref, gains_ref, *refs):
@@ -513,10 +513,10 @@
         k_gain_parts.append(k_gain_part)
         attended.append((parts, crossed_part))
 
-    everyone = cycle * lax.axis_size("heads")
+    sharers = lax.axis_size("heads")
     dq_raw, gains = pl.pallas_call(
         lambda *refs: query_kernel(blocks, inv_root, kv_heads, *refs),
-        out_shape=(sds((tokens, heads * head_dim), BF16), sds((everyone, 2, head_dim), F32)),
+        out_shape=(sds((tokens, heads * head_dim), BF16), sds((sharers, 2, head_dim), F32)),
         in_specs=[smem] + [vmem] * (6 + 2 * kv_heads),
         out_specs=(vmem, vmem),
         compiler_params=params,
@@ -549,12 +549,13 @@
             others = tree.across(near[None], [0], back=True)
         mine = [(parts[0], None), (others, 0)]
         terms.append(mine + [(tree.home(both, step), None) for both, step in zip(merged, steps)])
+    gains = lax.all_to_all(gains, "heads", 0, 0)
     for h in range(kv_heads):
         if h < kv_heads - 1:
             arrays, places = zip(*terms[h])
             early, gains = pl.pallas_call(
                 lambda *refs: early_kernel(places, *refs),
-                out_shape=(sds((tokens, 2 * head_dim), F32), sds(gains.shape, F32)),
+                out_shape=(sds((tokens, 2 * head_dim), F32), sds((cycle, 2, head_dim), F32)),
                 in_specs=[vmem] * (1 + len(arrays)),
                 out_specs=(vmem, vmem),
                 compiler_params=params,
@@ -563,7 +564,7 @@
             )(gains, *arrays)
             terms[h] = [(early, None)]
         terms[h].append((joined, h))
-    gains = lax.all_to_all(gains, ("ctx", "heads"), 0, 0)
+    gains = lax.all_to_all(gains, "ctx", 0, 0)
 
     arrays = [array for mine in terms for array, _ in mine]
     places = [[place for _, place in mine] for mine in terms]

time: 109 us -> 109 us (level)
  starting transfers between devices: 33.2 us -> 41.5 us
  Pallas kernels: 45.7 us -> 38.6 us
    pallas_call x2, Pallas kernels: 32.6 us -> 25 us  [attend(): pl.pallas_call(lambda *refs: main_kernel(blocks, block_len, tree_dev, inv...]
    ppermute x17, starting transfers between devices: 25.1 us -> 30.1 us  [send(): return lax.ppermute(value, 'ctx', pairs)]
    all_to_all x1 -> x2, starting transfers between devices: 8.11 us -> 11.3 us  [the longest x1 8.07 us: on_device(): gains = lax.all_to_all(gains, 'ctx', 0, 0)]
    all_to_all x1 -> x2, waiting for transfers between devices: 7.22 us -> 6.49 us  [the longest x1 6.49 us: on_device(): gains = lax.all_to_all(gains, 'ctx', 0, 0)]
  transfers between devices with their start and end apart: 18 -> 19, of which waited for: 5 -> 5; matrix products, arithmetic and copies ran while one was open for 1% -> 1% of each run, Pallas kernels for 41% -> 34%
where the time goes in v1:
time: 109 us
  starting transfers between devices  41.5 us (38%)
  Pallas kernels  38.6 us (35%)
  waiting for transfers between devices  21 us (19%)
  local copies, waits for them, and re-layouts  6.1 us (6%)
    ppermute x17, starting transfers between devices, send(): return lax.ppermute(value, 'ctx', pairs)  30.1 us
    pallas_call x2, Pallas kernels, attend(): pl.pallas_call(lambda *refs: main_kernel(blocks, block_len, tree_dev, inv...  25 us
    ppermute x17, waiting for transfers between devices, send(): return lax.ppermute(value, 'ctx', pairs)  14.5 us
    all_to_all x1, starting transfers between devices, on_device(): gains = lax.all_to_all(gains, 'ctx', 0, 0)  8.07 us
    all_to_all x1, waiting for transfers between devices, on_device(): gains = lax.all_to_all(gains, 'ctx', 0, 0)  6.49 us
    pallas_call x1, Pallas kernels, on_device(): pl.pallas_call(lambda *refs: query_kernel(blocks, inv_root, kv_heads, *re...  4.61 us
    unnamed x26, local copies, waits for them, and re-layouts  4.54 us
    pallas_call x1, Pallas kernels, on_device(): pl.pallas_call(lambda *refs: prep_kernel(blocks, block_len, kv_heads, *re...  4.08 us
  transfers between devices with their start and end apart: 19, of which 5 were waited for; matrix products, arithmetic and copies ran while one was open for 1% of the time, Pallas kernels for 34%

profile of v1, /device:TPU:0, one launch (start us, length us, event | category | flops | bytes accessed | tf_op | source)
XLA Modules:
  0.0 109.0 jit_solution(795399983164576186)
XLA Ops:
  0.6 1.0 fusion.7
  1.7 1.3 %collective-permute-start = (bf16[256,256]{1,0:T(8,128)(2,1)S(1)}, bf16[256,256]{1,0:T(8,128)(2,1)S(1)}, u32[]{:S(2)}, u32[]{:S(2)}) collective-permute-start(bf16[256,256]{1,0:T(8,128)(2,1)S(1)} %pad_maximum_fusion.refs_6_), channel_id=1, source_target_pairs={{4,12},{8,16},{12,20},{16,24},{20,28},{24,0},{28,4},{5,13},{9,17},... | collective-permute-start | bytes 393224 | tf_op jit(solution)/shard_map/ppermute | solution.py:357
  3.0 1.3 %collective-permute-start.1 = (bf16[256,256]{1,0:T(8,128)(2,1)S(1)}, bf16[256,256]{1,0:T(8,128)(2,1)S(1)}, u32[]{:S(2)}, u32[]{:S(2)}) collective-permute-start(bf16[256,256]{1,0:T(8,128)(2,1)S(1)} %pad_maximum_fusion.refs_6_), channel_id=1, source_target_pairs={{4,20},{8,24},{12,28},{16,0},{20,4},{5,21},{9,25},{13,29},{17,1},{... | collective-permute-start | bytes 393224 | tf_op jit(solution)/shard_map/ppermute | solution.py:357
  4.3 1.3 %collective-permute-start.2 = (bf16[256,256]{1,0:T(8,128)(2,1)S(1)}, bf16[256,256]{1,0:T(8,128)(2,1)S(1)}, u32[]{:S(2)}, u32[]{:S(2)}) collective-permute-start(bf16[256,256]{1,0:T(8,128)(2,1)S(1)} %pad_maximum_fusion.refs_6_), channel_id=1, source_target_pairs={{4,28},{8,0},{12,4},{5,29},{9,1},{13,5},{6,30},{10,2},{14,6},{7,31... | collective-permute-start | bytes 393224 | tf_op jit(solution)/shard_map/ppermute | solution.py:357
  5.6 1.3 %collective-permute-start.3 = (bf16[256,256]{1,0:T(8,128)(2,1)S(1)}, bf16[256,256]{1,0:T(8,128)(2,1)S(1)}, u32[]{:S(2)}, u32[]{:S(2)}) collective-permute-start(bf16[256,256]{1,0:T(8,128)(2,1)S(1)} %pad_maximum_fusion.refs_6_), channel_id=1, source_target_pairs={{4,0},{8,12},{16,20},{24,28},{5,1},{9,13},{17,21},{25,29},{6,2},{1... | collective-permute-start | bytes 393224 | tf_op jit(solution)/shard_map/ppermute | solution.py:357
  6.9 1.3 %collective-permute-start.5 = (bf16[256,256]{1,0:T(8,128)(2,1)S(1)}, bf16[256,256]{1,0:T(8,128)(2,1)S(1)}, u32[]{:S(2)}, u32[]{:S(2)}) collective-permute-start(bf16[256,256]{1,0:T(8,128)(2,1)S(1)} %pad_maximum_fusion.1.refs_0_.refs_6_), channel_id=1, source_target_pairs={{4,12},{8,16},{12,20},{16,24},{20,28},{24,0},{28,4},{5,13},{9,17},... | collective-permute-start | bytes 393224 | tf_op jit(solution)/shard_map/ppermute | solution.py:357
  8.3 0.0 copy-start.12
  8.3 0.7 copy-done.12
  8.9 0.7 fusion.6
  9.7 2.0 %plan.1.refs_4_.refs_0_ = s32[5,32]{1,0:T(8,128)} custom-call(s32[1]{0:T(128)} %bitcast.1.refs_0_, s32[4,32]{1,0:T(4,128)} %get-tuple-element.86.refs_1_), custom_call_target="tpu_custom_call" | custom-call | flops 1024 | bytes 1024 | tf_op jit(solution)/shard_map/plan/pallas_call | solution.py:420
  11.7 0.0 copy-start.2
  11.7 0.0 copy-start.3
  11.7 0.0 copy-start.4
  11.7 0.0 copy-start.5
  11.7 0.5 collective-permute-done.refs_0_.refs_7_
  12.3 1.3 %collective-permute-start.6 = (bf16[256,256]{1,0:T(8,128)(2,1)S(1)}, bf16[256,256]{1,0:T(8,128)(2,1)S(1)}, u32[]{:S(2)}, u32[]{:S(2)}) collective-permute-start(bf16[256,256]{1,0:T(8,128)(2,1)S(1)} %pad_maximum_fusion.1.refs_0_.refs_6_), channel_id=1, source_target_pairs={{4,20},{8,24},{12,28},{16,0},{20,4},{5,21},{9,25},{13,29},{17,1},{... | collective-permute-start | bytes 393224 | tf_op jit(solution)/shard_map/ppermute | solution.py:357
  13.5 1.5 %collective-permute-done.1.refs_1_.refs_8_ = bf16[256,256]{1,0:T(8,128)(2,1)S(1)} collective-permute-done((bf16[256,256]{1,0:T(8,128)(2,1)S(1)}, bf16[256,256]{1,0:T(8,128)(2,1)S(1)}, u32[]{:S(2)}, u32[]{:S(2)}) %collective-permute-start.1) | collective-permute-done | bytes 131104 | tf_op jit(solution)/shard_map/ppermute | solution.py:357
  15.1 1.3 %collective-permute-start.7 = (bf16[256,256]{1,0:T(8,128)(2,1)S(1)}, bf16[256,256]{1,0:T(8,128)(2,1)S(1)}, u32[]{:S(2)}, u32[]{:S(2)}) collective-permute-start(bf16[256,256]{1,0:T(8,128)(2,1)S(1)} %pad_maximum_fusion.1.refs_0_.refs_6_), channel_id=1, source_target_pairs={{4,28},{8,0},{12,4},{5,29},{9,1},{13,5},{6,30},{10,2},{14,6},{7,31... | collective-permute-start | bytes 393224 | tf_op jit(solution)/shard_map/ppermute | solution.py:357
  16.4 4.2 %collective-permute-done.2.refs_2_.refs_9_ = bf16[256,256]{1,0:T(8,128)(2,1)S(1)} collective-permute-done((bf16[256,256]{1,0:T(8,128)(2,1)S(1)}, bf16[256,256]{1,0:T(8,128)(2,1)S(1)}, u32[]{:S(2)}, u32[]{:S(2)}) %collective-permute-start.2) | collective-permute-done | bytes 131104 | tf_op jit(solution)/shard_map/ppermute | solution.py:357
  20.6 0.7 copy-done.6
  21.3 0.0 copy-start.8
  21.3 1.3 %collective-permute-start.4 = (bf16[3,256,256]{2,1,0:T(8,128)(2,1)S(1)}, bf16[3,256,256]{2,1,0:T(8,128)(2,1)S(1)}, u32[]{:S(2)}, u32[]{:S(2)}) collective-permute-start(bf16[3,256,256]{2,1,0:T(8,128)(2,1)S(1)} %join.2), channel_id=1, source_target_pairs={{4,0},{12,8},{16,20},{20,16},{24,28},{28,24},{5,1},{13,9},{17,21},... | collective-permute-start | bytes 1179656 | tf_op jit(solution)/shard_map/ppermute | solution.py:357
  22.7 0.0 copy-start.10
  22.7 1.2 %copy-done.10 = bf16[256,2048]{1,0:T(8,128)(2,1)S(1)} copy-done((bf16[256,2048]{1,0:T(8,128)(2,1)S(1)}, bf16[256,2048]{1,0:T(8,128)(2,1)}, u32[]{:S(2)}) %copy-start.10) | copy-done | bytes 1048600
  23.9 1.2 %copy-done.11 = bf16[256,2048]{1,0:T(8,128)(2,1)S(1)} copy-done((bf16[256,2048]{1,0:T(8,128)(2,1)S(1)}, bf16[256,2048]{1,0:T(8,128)(2,1)}, u32[]{:S(2)}) %copy-start.11) | copy-done | bytes 1048600
  25.1 4.1 %prep.1 = (bf16[128,2048]{1,0:T(8,128)(2,1)S(1)}, bf16[2048,128]{1,0:T(8,128)(2,1)S(1)}, bf16[128,2048]{1,0:T(8,128)(2,1)S(1)}, bf16[2048,128]{1,0:T(8,128)(2,1)...) custom-call(s32[4]{0:T(128)S(1)} %broadcast_add_fusion.refs_0_, ...), custom_call_target="tpu_custom_call" | custom-call | flops 4000000000 | bytes 16777216 | tf_op jit(solution)/shard_map/prep/pallas_call | solution.py:442
  29.3 1.3 %collective-permute-start.8 = (bf16[4,256,256]{2,1,0:T(8,128)(2,1)S(1)}, bf16[4,256,256]{2,1,0:T(8,128)(2,1)S(1)}, u32[]{:S(2)}, u32[]{:S(2)}) collective-permute-start(bf16[4,256,256]{2,1,0:T(8,128)(2,1)S(1)} %join.3), channel_id=1, source_target_pairs={{4,0},{8,12},{12,8},{16,20},{20,16},{24,28},{28,24},{5,1},{9,13},{... | collective-permute-start | bytes 1572872 | tf_op jit(solution)/shard_map/ppermute | solution.py:357
  30.6 8.2 %collective-permute-done.4.refs_11_ = bf16[3,256,256]{2,1,0:T(8,128)(2,1)S(1)} collective-permute-done((bf16[3,256,256]{2,1,0:T(8,128)(2,1)S(1)}, bf16[3,256,256]{2,1,0:T(8,128)(2,1)S(1)}, u32[]{:S(2)}, u32[]{:S(2)}) %collective-permute-start.4) | collective-permute-done | bytes 393248 | tf_op jit(solution)/shard_map/ppermute | solution.py:357
  38.8 0.7 copy-done.7
  39.5 12.4 %attend.2 = (f32[128,2048]{1,0:T(8,128)S(1)}, f32[8,128]{1,0:T(8,128)S(1)}, bf16[256,256]{1,0:T(8,128)(2,1)S(1)}, bf16[256,256]{1,0:T(8,128)(2,1)S(1)}, bf16[256...) custom-call(s32[5,32]{1,0:T(8,128)S(1)} %copy-done.7, f32[1,128]{1,0:T(1,128)S(1)} %bitcast.27, ...), custom_call_target="tpu_custom_call" | custom-call | flops 5368709120 | bytes 8388608 | tf_op jit(solution)/shard_map/attend/pallas_call | solution.py:476
  51.9 1.5 %collective-permute-start.10 = (bf16[4,256,256]{2,1,0:T(8,128)(2,1)S(1)}, bf16[4,256,256]{2,1,0:T(8,128)(2,1)S(1)}, u32[]{:S(2)}, u32[]{:S(2)}) collective-permute-start(bf16[4,256,256]{2,1,0:T(8,128)(2,1)S(1)} %get-tuple-element.64), channel_id=1, source_target_pairs={{0,4},{8,12},{12,8},{16,20},{20,16},{24,28},{28,24},{1,5},{9,13},{... | collective-permute-start | bytes 1572872 | tf_op jit(solution)/shard_map/ppermute | solution.py:357
  53.4 12.5 %attend.3 = (f32[128,2048]{1,0:T(8,128)S(1)}, f32[8,128]{1,0:T(8,128)S(1)}, bf16[256,256]{1,0:T(8,128)(2,1)S(1)}, bf16[256,256]{1,0:T(8,128)(2,1)S(1)}, bf16[256...) custom-call(s32[5,32]{1,0:T(8,128)S(1)} %copy-done.7, ...), custom_call_target="tpu_custom_call" | custom-call | flops 5368709120 | bytes 8388608 | tf_op jit(solution)/shard_map/attend/pallas_call | solution.py:476
  65.9 1.3 %collective-permute-start.9 = (bf16[3,256,256]{2,1,0:T(8,128)(2,1)S(1)}, bf16[3,256,256]{2,1,0:T(8,128)(2,1)S(1)}, u32[]{:S(2)}, u32[]{:S(2)}) collective-permute-start(bf16[3,256,256]{2,1,0:T(8,128)(2,1)S(1)} %get-tuple-element.61), channel_id=1, source_target_pairs={{0,4},{8,12},{16,20},{20,16},{24,28},{28,24},{1,5},{9,13},{17,21},... | collective-permute-start | bytes 1179656 | tf_op jit(solution)/shard_map/ppermute | solution.py:357
  67.3 0.1 fusion
  67.4 5.4 %collective-permute-start.11 = (bf16[256,256]{1,0:T(8,128)(2,1)S(1)}, bf16[256,256]{1,0:T(8,128)(2,1)S(1)}, u32[]{:S(2)}, u32[]{:S(2)}) collective-permute-start(bf16[256,256]{1,0:T(8,128)(2,1)S(1)} %get-tuple-element.80), channel_id=1, source_target_pairs={{0,24},{4,28},{12,4},{16,8},{20,12},{24,16},{28,20},{1,25},{5,29},... | collective-permute-start | bytes 393224 | tf_op jit(solution)/shard_map/ppermute | solution.py:357
  72.8 1.3 %collective-permute-start.12 = (bf16[256,256]{1,0:T(8,128)(2,1)S(1)}, bf16[256,256]{1,0:T(8,128)(2,1)S(1)}, u32[]{:S(2)}, u32[]{:S(2)}) collective-permute-start(bf16[256,256]{1,0:T(8,128)(2,1)S(1)} %get-tuple-element.79), channel_id=1, source_target_pairs={{0,16},{4,20},{20,4},{24,8},{28,12},{1,17},{5,21},{21,5},{25,9},{2... | collective-permute-start | bytes 393224 | tf_op jit(solution)/shard_map/ppermute | solution.py:357
  74.1 4.6 %query_back.1 = (bf16[256,2048]{1,0:T(8,128)(2,1)}, f32[4,2,128]{2,1,0:T(2,128)S(1)}) custom-call(s32[4]{0:T(128)S(1)} %broadcast_add_fusion.refs_0_, f32[32,128]{1,0:T(8,128)S(1)} %copy-done.4, f32[32,128]{1,0:T(8,128)S(1)} %copy-done.5, f32[64,128]{1,0:T(8,128)S(1)} %copy-done.2, f32[64,128]{1,0:T(8,128)S(1)} %copy-done.3, f32[1,128]{1,0:T(1,128)S(1)} %bitcast.26, ...), custom_call_target="tpu_custom_call" | custom-call | tf_op jit(solution)/shard_map/query_back/pallas_call | solution.py:517
  78.7 0.7 merge.1
  79.3 3.2 %all-to-all-start = ((f32[4,2,128]{2,1,0:T(2,128)}), f32[4,2,128]{2,1,0:T(2,128)S(1)}, u32[]{:S(2)}, u32[]{:S(2)}) async-start(f32[4,2,128]{2,1,0:T(2,128)} %get-tuple-element.65), calls=%async_computation | async-start | bytes 8192 | tf_op jit(solution)/shard_map/all_to_all | solution.py:552
  82.6 1.3 %collective-permute-start.13 = (bf16[2,256,256]{2,1,0:T(8,128)(2,1)S(1)}, bf16[2,256,256]{2,1,0:T(8,128)(2,1)S(1)}, u32[]{:S(2)}, u32[]{:S(2)}) collective-permute-start(bf16[2,256,256]{2,1,0:T(8,128)(2,1)S(1)} %get-tuple-element.71), channel_id=1, source_target_pairs={{0,8},{4,12},{28,4},{1,9},{5,13},{29,5},{2,10},{6,14},{30,6},{3,11... | collective-permute-start | bytes 786440 | tf_op jit(solution)/shard_map/ppermute | solution.py:357
  83.9 5.2 %collective-permute-start.14 = (bf16[1,256,256]{2,1,0:T(8,128)(2,1)S(1)}, bf16[1,256,256]{2,1,0:T(8,128)(2,1)S(1)}, u32[]{:S(2)}, u32[]{:S(2)}) collective-permute-start(bf16[1,256,256]{2,1,0:T(8,128)(2,1)S(1)} %bitcast.30), channel_id=1, source_target_pairs={{0,4},{12,8},{20,16},{28,24},{1,5},{13,9},{21,17},{29,25},{2,6},{1... | collective-permute-start | bytes 393224 | tf_op jit(solution)/shard_map/ppermute | solution.py:357
  89.1 1.3 %collective-permute-start.15 = (bf16[256,256]{1,0:T(8,128)(2,1)S(1)}, bf16[256,256]{1,0:T(8,128)(2,1)S(1)}, u32[]{:S(2)}, u32[]{:S(2)}) collective-permute-start(bf16[256,256]{1,0:T(8,128)(2,1)S(1)} %get-tuple-element.74), channel_id=1, source_target_pairs={{0,24},{4,28},{12,4},{16,8},{20,12},{24,16},{28,20},{1,25},{5,29},... | collective-permute-start | bytes 393224 | tf_op jit(solution)/shard_map/ppermute | solution.py:357
  90.4 1.3 %collective-permute-start.16 = (bf16[256,256]{1,0:T(8,128)(2,1)S(1)}, bf16[256,256]{1,0:T(8,128)(2,1)S(1)}, u32[]{:S(2)}, u32[]{:S(2)}) collective-permute-start(bf16[256,256]{1,0:T(8,128)(2,1)S(1)} %get-tuple-element.75), channel_id=1, source_target_pairs={{0,16},{4,20},{20,4},{24,8},{28,12},{1,17},{5,21},{21,5},{25,9},{2... | collective-permute-start | bytes 393224 | tf_op jit(solution)/shard_map/ppermute | solution.py:357
  91.7 0.6 early.1
  92.3 8.1 %all-to-all-start.1 = ((f32[8,2,128]{2,1,0:T(2,128)}), f32[8,2,128]{2,1,0:T(2,128)S(1)}, u32[]{:S(2)}, u32[]{:S(2)}) async-start(f32[8,2,128]{2,1,0:T(2,128)} %get-tuple-element.69), calls=%async_computation.1 | async-start | bytes 16384 | tf_op jit(solution)/shard_map/all_to_all | solution.py:567
  100.4 6.5 %all-to-all-done.1.refs_7_ = f32[8,2,128]{2,1,0:T(2,128)S(1)} async-done(((f32[8,2,128]{2,1,0:T(2,128)}), f32[8,2,128]{2,1,0:T(2,128)S(1)}, u32[]{:S(2)}, u32[]{:S(2)}) %all-to-all-start.1) | async-done | bytes 8224 | tf_op jit(solution)/shard_map/all_to_all | solution.py:567
  106.9 1.6 %key_back.1 = (bf16[256,256]{1,0:T(8,128)(2,1)}, bf16[256,256]{1,0:T(8,128)(2,1)}, f32[2,128]{1,0:T(2,128)S(1)}) custom-call(s32[4]{0:T(128)S(1)} %broadcast_add_fusion.refs_0_, f32[32,128]{1,0:T(8,128)S(1)} %copy-done.4, f32[32,128]{1,0:T(8,128)S(1)} %copy-done.5, f32[64,128]{1,0:T(8,128)S(1)} %copy-done.2, f32[64,128]{1,0:T(8,128)S(1)} %copy-done.3, ...), custom_call_target="tpu_custom_call" | custom-call | tf_op jit(solution)/shard_map/key_back/pallas_call | solution.py:571
  108.5 0.5 slice_bitcast_fusion.3
  (33 shorter events, 0.2 us)
Async XLA Ops:
  0.6 22.0 %copy-start = (bf16[256,2048]{1,0:T(8,128)(2,1)S(1)}, bf16[256,2048]{1,0:T(8,128)(2,1)}, u32[]{:S(2)}) copy-start(bf16[256,2048]{1,0:T(8,128)(2,1)} %refs_6_.4) | copy-start | bytes 3145732
  1.7 10.5 %collective-permute-start = (bf16[256,256]{1,0:T(8,128)(2,1)S(1)}, bf16[256,256]{1,0:T(8,128)(2,1)S(1)}, u32[]{:S(2)}, u32[]{:S(2)}) collective-permute-start(bf16[256,256]{1,0:T(8,128)(2,1)S(1)} %pad_maximum_fusion.refs_6_), channel_id=1, source_target_pairs={{4,12},{8,16},{12,20},{16,24},{20,28},{24,0},{28,4},{5,13},{9,17},... | collective-permute-start | bytes 393224 | tf_op jit(solution)/shard_map/ppermute | solution.py:357
  3.0 12.1 %collective-permute-start.1 = (bf16[256,256]{1,0:T(8,128)(2,1)S(1)}, bf16[256,256]{1,0:T(8,128)(2,1)S(1)}, u32[]{:S(2)}, u32[]{:S(2)}) collective-permute-start(bf16[256,256]{1,0:T(8,128)(2,1)S(1)} %pad_maximum_fusion.refs_6_), channel_id=1, source_target_pairs={{4,20},{8,24},{12,28},{16,0},{20,4},{5,21},{9,25},{13,29},{17,1},{... | collective-permute-start | bytes 393224 | tf_op jit(solution)/shard_map/ppermute | solution.py:357
  4.3 16.3 %collective-permute-start.2 = (bf16[256,256]{1,0:T(8,128)(2,1)S(1)}, bf16[256,256]{1,0:T(8,128)(2,1)S(1)}, u32[]{:S(2)}, u32[]{:S(2)}) collective-permute-start(bf16[256,256]{1,0:T(8,128)(2,1)S(1)} %pad_maximum_fusion.refs_6_), channel_id=1, source_target_pairs={{4,28},{8,0},{12,4},{5,29},{9,1},{13,5},{6,30},{10,2},{14,6},{7,31... | collective-permute-start | bytes 393224 | tf_op jit(solution)/shard_map/ppermute | solution.py:357
  5.6 15.0 %collective-permute-start.3 = (bf16[256,256]{1,0:T(8,128)(2,1)S(1)}, bf16[256,256]{1,0:T(8,128)(2,1)S(1)}, u32[]{:S(2)}, u32[]{:S(2)}) collective-permute-start(bf16[256,256]{1,0:T(8,128)(2,1)S(1)} %pad_maximum_fusion.refs_6_), channel_id=1, source_target_pairs={{4,0},{8,12},{16,20},{24,28},{5,1},{9,13},{17,21},{25,29},{6,2},{1... | collective-permute-start | bytes 393224 | tf_op jit(solution)/shard_map/ppermute | solution.py:357
  6.9 22.3 %collective-permute-start.5 = (bf16[256,256]{1,0:T(8,128)(2,1)S(1)}, bf16[256,256]{1,0:T(8,128)(2,1)S(1)}, u32[]{:S(2)}, u32[]{:S(2)}) collective-permute-start(bf16[256,256]{1,0:T(8,128)(2,1)S(1)} %pad_maximum_fusion.1.refs_0_.refs_6_), channel_id=1, source_target_pairs={{4,12},{8,16},{12,20},{16,24},{20,28},{24,0},{28,4},{5,13},{9,17},... | collective-permute-start | bytes 393224 | tf_op jit(solution)/shard_map/ppermute | solution.py:357
  8.3 0.7 copy-start.12
  11.7 11.0 %copy-start.2 = (f32[64,128]{1,0:T(8,128)S(1)}, f32[64,128]{1,0:T(8,128)}, u32[]{:S(2)}) copy-start(f32[64,128]{1,0:T(8,128)} %constant.66.clone.refs_3_.refs_4_) | copy-start | bytes 98308
  11.7 10.9 %copy-start.3 = (f32[64,128]{1,0:T(8,128)S(1)}, f32[64,128]{1,0:T(8,128)}, u32[]{:S(2)}) copy-start(f32[64,128]{1,0:T(8,128)} %constant.67.clone.refs_4_.refs_5_) | copy-start | bytes 98308
  11.7 10.9 %copy-start.4 = (f32[32,128]{1,0:T(8,128)S(1)}, f32[32,128]{1,0:T(8,128)}, u32[]{:S(2)}) copy-start(f32[32,128]{1,0:T(8,128)} %constant.64.clone.refs_1_.refs_2_) | copy-start | bytes 49156
  11.7 10.9 %copy-start.5 = (f32[32,128]{1,0:T(8,128)S(1)}, f32[32,128]{1,0:T(8,128)}, u32[]{:S(2)}) copy-start(f32[32,128]{1,0:T(8,128)} %constant.65.clone.refs_2_.refs_3_) | copy-start | bytes 49156
  12.3 17.0 %collective-permute-start.6 = (bf16[256,256]{1,0:T(8,128)(2,1)S(1)}, bf16[256,256]{1,0:T(8,128)(2,1)S(1)}, u32[]{:S(2)}, u32[]{:S(2)}) collective-permute-start(bf16[256,256]{1,0:T(8,128)(2,1)S(1)} %pad_maximum_fusion.1.refs_0_.refs_6_), channel_id=1, source_target_pairs={{4,20},{8,24},{12,28},{16,0},{20,4},{5,21},{9,25},{13,29},{17,1},{... | collective-permute-start | bytes 393224 | tf_op jit(solution)/shard_map/ppermute | solution.py:357
  15.1 14.2 %collective-permute-start.7 = (bf16[256,256]{1,0:T(8,128)(2,1)S(1)}, bf16[256,256]{1,0:T(8,128)(2,1)S(1)}, u32[]{:S(2)}, u32[]{:S(2)}) collective-permute-start(bf16[256,256]{1,0:T(8,128)(2,1)S(1)} %pad_maximum_fusion.1.refs_0_.refs_6_), channel_id=1, source_target_pairs={{4,28},{8,0},{12,4},{5,29},{9,1},{13,5},{6,30},{10,2},{14,6},{7,31... | collective-permute-start | bytes 393224 | tf_op jit(solution)/shard_map/ppermute | solution.py:357
  20.6 0.7 copy-start.6
  21.3 1.4 %copy-start.8 = (f32[128]{0:T(128)S(1)}, f32[128]{0:T(128)}, u32[]{:S(2)}) copy-start(f32[128]{0:T(128)} %param.17) | copy-start | bytes 1540
  21.3 17.4 %collective-permute-start.4 = (bf16[3,256,256]{2,1,0:T(8,128)(2,1)S(1)}, bf16[3,256,256]{2,1,0:T(8,128)(2,1)S(1)}, u32[]{:S(2)}, u32[]{:S(2)}) collective-permute-start(bf16[3,256,256]{2,1,0:T(8,128)(2,1)S(1)} %join.2), channel_id=1, source_target_pairs={{4,0},{12,8},{16,20},{20,16},{24,28},{28,24},{5,1},{13,9},{17,21},... | collective-permute-start | bytes 1179656 | tf_op jit(solution)/shard_map/ppermute | solution.py:357
  22.7 1.2 %copy-start.10 = (bf16[256,2048]{1,0:T(8,128)(2,1)S(1)}, bf16[256,2048]{1,0:T(8,128)(2,1)}, u32[]{:S(2)}) copy-start(bf16[256,2048]{1,0:T(8,128)(2,1)} %refs_7_.1) | copy-start | bytes 3145732
  23.9 1.2 %copy-start.11 = (bf16[256,2048]{1,0:T(8,128)(2,1)S(1)}, bf16[256,2048]{1,0:T(8,128)(2,1)}, u32[]{:S(2)}) copy-start(bf16[256,2048]{1,0:T(8,128)(2,1)} %refs_8_.1) | copy-start | bytes 3145732
  29.3 24.1 %collective-permute-start.8 = (bf16[4,256,256]{2,1,0:T(8,128)(2,1)S(1)}, bf16[4,256,256]{2,1,0:T(8,128)(2,1)S(1)}, u32[]{:S(2)}, u32[]{:S(2)}) collective-permute-start(bf16[4,256,256]{2,1,0:T(8,128)(2,1)S(1)} %join.3), channel_id=1, source_target_pairs={{4,0},{8,12},{12,8},{16,20},{20,16},{24,28},{28,24},{5,1},{9,13},{... | collective-permute-start | bytes 1572872 | tf_op jit(solution)/shard_map/ppermute | solution.py:357
  38.8 0.7 copy-start.7
  38.8 0.7 copy-start.9
  51.9 15.4 %collective-permute-start.10 = (bf16[4,256,256]{2,1,0:T(8,128)(2,1)S(1)}, bf16[4,256,256]{2,1,0:T(8,128)(2,1)S(1)}, u32[]{:S(2)}, u32[]{:S(2)}) collective-permute-start(bf16[4,256,256]{2,1,0:T(8,128)(2,1)S(1)} %get-tuple-element.64), channel_id=1, source_target_pairs={{0,4},{8,12},{12,8},{16,20},{20,16},{24,28},{28,24},{1,5},{9,13},{... | collective-permute-start | bytes 1572872 | tf_op jit(solution)/shard_map/ppermute | solution.py:357
  65.9 12.7 %collective-permute-start.9 = (bf16[3,256,256]{2,1,0:T(8,128)(2,1)S(1)}, bf16[3,256,256]{2,1,0:T(8,128)(2,1)S(1)}, u32[]{:S(2)}, u32[]{:S(2)}) collective-permute-start(bf16[3,256,256]{2,1,0:T(8,128)(2,1)S(1)} %get-tuple-element.61), channel_id=1, source_target_pairs={{0,4},{8,12},{16,20},{20,16},{24,28},{28,24},{1,5},{9,13},{17,21},... | collective-permute-start | bytes 1179656 | tf_op jit(solution)/shard_map/ppermute | solution.py:357
  67.4 23.0 %collective-permute-start.11 = (bf16[256,256]{1,0:T(8,128)(2,1)S(1)}, bf16[256,256]{1,0:T(8,128)(2,1)S(1)}, u32[]{:S(2)}, u32[]{:S(2)}) collective-permute-start(bf16[256,256]{1,0:T(8,128)(2,1)S(1)} %get-tuple-element.80), channel_id=1, source_target_pairs={{0,24},{4,28},{12,4},{16,8},{20,12},{24,16},{28,20},{1,25},{5,29},... | collective-permute-start | bytes 393224 | tf_op jit(solution)/shard_map/ppermute | solution.py:357
  72.8 18.9 %collective-permute-start.12 = (bf16[256,256]{1,0:T(8,128)(2,1)S(1)}, bf16[256,256]{1,0:T(8,128)(2,1)S(1)}, u32[]{:S(2)}, u32[]{:S(2)}) collective-permute-start(bf16[256,256]{1,0:T(8,128)(2,1)S(1)} %get-tuple-element.79), channel_id=1, source_target_pairs={{0,16},{4,20},{20,4},{24,8},{28,12},{1,17},{5,21},{21,5},{25,9},{2... | collective-permute-start | bytes 393224 | tf_op jit(solution)/shard_map/ppermute | solution.py:357
  79.3 12.4 %all-to-all-start = ((f32[4,2,128]{2,1,0:T(2,128)}), f32[4,2,128]{2,1,0:T(2,128)S(1)}, u32[]{:S(2)}, u32[]{:S(2)}) async-start(f32[4,2,128]{2,1,0:T(2,128)} %get-tuple-element.65), calls=%async_computation | async-start | bytes 8192 | tf_op jit(solution)/shard_map/all_to_all | solution.py:552
  82.6 24.3 %collective-permute-start.13 = (bf16[2,256,256]{2,1,0:T(8,128)(2,1)S(1)}, bf16[2,256,256]{2,1,0:T(8,128)(2,1)S(1)}, u32[]{:S(2)}, u32[]{:S(2)}) collective-permute-start(bf16[2,256,256]{2,1,0:T(8,128)(2,1)S(1)} %get-tuple-element.71), channel_id=1, source_target_pairs={{0,8},{4,12},{28,4},{1,9},{5,13},{29,5},{2,10},{6,14},{30,6},{3,11... | collective-permute-start | bytes 786440 | tf_op jit(solution)/shard_map/ppermute | solution.py:357
  83.9 16.5 %collective-permute-start.14 = (bf16[1,256,256]{2,1,0:T(8,128)(2,1)S(1)}, bf16[1,256,256]{2,1,0:T(8,128)(2,1)S(1)}, u32[]{:S(2)}, u32[]{:S(2)}) collective-permute-start(bf16[1,256,256]{2,1,0:T(8,128)(2,1)S(1)} %bitcast.30), channel_id=1, source_target_pairs={{0,4},{12,8},{20,16},{28,24},{1,5},{13,9},{21,17},{29,25},{2,6},{1... | collective-permute-start | bytes 393224 | tf_op jit(solution)/shard_map/ppermute | solution.py:357
  89.1 11.4 %collective-permute-start.15 = (bf16[256,256]{1,0:T(8,128)(2,1)S(1)}, bf16[256,256]{1,0:T(8,128)(2,1)S(1)}, u32[]{:S(2)}, u32[]{:S(2)}) collective-permute-start(bf16[256,256]{1,0:T(8,128)(2,1)S(1)} %get-tuple-element.74), channel_id=1, source_target_pairs={{0,24},{4,28},{12,4},{16,8},{20,12},{24,16},{28,20},{1,25},{5,29},... | collective-permute-start | bytes 393224 | tf_op jit(solution)/shard_map/ppermute | solution.py:357
  90.4 10.1 %collective-permute-start.16 = (bf16[256,256]{1,0:T(8,128)(2,1)S(1)}, bf16[256,256]{1,0:T(8,128)(2,1)S(1)}, u32[]{:S(2)}, u32[]{:S(2)}) collective-permute-start(bf16[256,256]{1,0:T(8,128)(2,1)S(1)} %get-tuple-element.75), channel_id=1, source_target_pairs={{0,16},{4,20},{20,4},{24,8},{28,12},{1,17},{5,21},{21,5},{25,9},{2... | collective-permute-start | bytes 393224 | tf_op jit(solution)/shard_map/ppermute | solution.py:357
  91.7 15.2 %copy-start.1 = (bf16[256,256]{1,0:T(8,128)(2,1)S(1)}, bf16[256,256]{1,0:T(8,128)(2,1)}, u32[]{:S(2)}) copy-start(bf16[256,256]{1,0:T(8,128)(2,1)} %refs_6_.5) | copy-start | bytes 393220
  92.3 14.6 %all-to-all-start.1 = ((f32[8,2,128]{2,1,0:T(2,128)}), f32[8,2,128]{2,1,0:T(2,128)S(1)}, u32[]{:S(2)}, u32[]{:S(2)}) async-start(f32[8,2,128]{2,1,0:T(2,128)} %get-tuple-element.69), calls=%async_computation.1 | async-start | bytes 16384 | tf_op jit(solution)/shard_map/all_to_all | solution.py:567
